TPU v7x, 32 devices: a whole 2x2x4 slice. The times are simulated.
32 devices in a mesh: ep: 8 (over z, x), tp: 4 (over y, core).
Axes of the slice: x: 2, y: 2, z: 4, core: 2. Of those that a mesh axis runs over, the one named last changes fastest.
Arguments:
- tokens: bfloat16 [2048, 3072], P('ep', 'tp'), may hold values from -6 to 6
- routes: int32 [2048, 2], P('ep'), may hold values from 0 to 7, as said below
- route_gates: float32 [2048, 2], P('ep'), may hold values from 0.1 to 1
- up_weight: bfloat16 [8, 3072, 8192], P('ep', None, 'tp'), may hold values from -0.109375 to 0.109375
- down_weight: bfloat16 [8, 8192, 3072], P('ep', 'tp'), may hold values from -0.0625 to 0.0625
Outputs:
- layer_output: bfloat16 [2048, 3072], P('ep', 'tp')
Inputs may be any that keep to these rules, and one draw needn't show every extreme that they name: `routes`: each row names two different experts. Among the 256 rows of one index of ep no expert is named more than 128 times, and one expert is named exactly 128 times by the rows of every index of ep.
All inputs are finite; a program needn't handle non-finite values.
Results may differ from a plain program's by a relative error of at most 0.019.
Values may be sent and summed in bfloat16 or wider, within the bound.
No kernel may reach another device: no remote copies, remote signals or barrier semaphores. Data moves between devices by JAX's collectives and lax.ppermute only.
A program may use at most 64 MiB of HBM per device.

v0:
```python
import jax
import jax.numpy as jnp
from jax import lax
from jax.sharding import PartitionSpec as P


def slot_tables(routes, experts, slot_size):
    token_count = routes.shape[0]
    flat_routes = routes.reshape(token_count * 2)
    member = (flat_routes[:, None] == jnp.arange(experts, dtype=jnp.int32)[None, :]).astype(
        jnp.int32
    )
    before = jnp.cumsum(member, axis=0) - member
    position = jnp.sum(before * member, axis=1)
    target = flat_routes * slot_size + position
    capacity = experts * slot_size
    matches = jnp.arange(capacity, dtype=jnp.int32)[:, None] == target[None, :]
    owners = jnp.arange(token_count * 2, dtype=jnp.int32) // 2
    filled = jnp.any(matches, axis=1)
    source = jnp.sum(jnp.where(matches, owners[None, :], 0), axis=1)
    return (target.reshape(token_count, 2), source, filled)


def per_device(tokens, routes, route_gates, up_weight, down_weight):
    experts = lax.axis_size("ep")
    token_count = tokens.shape[0]
    slot_size = 4 * token_count // experts
    capacity = experts * slot_size
    target, source, filled = slot_tables(routes, experts, slot_size)
    up_matrix = up_weight[0]
    down_matrix = down_weight[0]
    portion = lax.all_gather(tokens, "tp", axis=1, tiled=True)
    outgoing = jnp.where(filled[:, None], portion[source], jnp.zeros((), portion.dtype))
    outgoing = outgoing.reshape(experts, slot_size, outgoing.shape[1])
    arrived = lax.all_to_all(outgoing, "ep", split_axis=0, concat_axis=0, tiled=True)
    arrived = arrived.reshape(capacity, arrived.shape[2])
    raised = jnp.dot(arrived, up_matrix, preferred_element_type=jnp.float32)
    hidden = jax.nn.silu(raised).astype(jnp.bfloat16)
    partial_value = jnp.dot(hidden, down_matrix, preferred_element_type=jnp.float32)
    summed = lax.psum_scatter(
        partial_value.astype(jnp.bfloat16), "tp", scatter_dimension=1, tiled=True
    ).astype(jnp.float32)
    result = summed.astype(jnp.bfloat16).reshape(experts, slot_size, summed.shape[1])
    returned = lax.all_to_all(result, "ep", split_axis=0, concat_axis=0, tiled=True)
    returned = returned.reshape(capacity, summed.shape[1])
    first_pick = returned[target[:, 0]].astype(jnp.float32)
    second_pick = returned[target[:, 1]].astype(jnp.float32)
    combined = route_gates[:, 0:1] * first_pick + route_gates[:, 1:2] * second_pick
    return combined.astype(jnp.bfloat16)


def solution(mesh):
    in_specs = (
        P("ep", "tp"),
        P("ep", None),
        P("ep", None),
        P("ep", None, "tp"),
        P("ep", "tp", None),
    )
    out_specs = P("ep", "tp")
    return jax.shard_map(
        per_device, mesh=mesh, in_specs=in_specs, out_specs=out_specs, check_vma=False
    )
```

profile of v0, /device:TPU:0, one launch (start us, length us, event | category | flops | bytes accessed | tf_op | source)
XLA Modules:
  0.0 339.5 jit_solution(5470576937638524879)
XLA Ops:
  6.5 0.0 all-gather.2.cloned.1.call-start
  6.5 0.7 all-gather.2.cloned.1.call-update
  7.3 0.0 reduce-scatter.2.cloned.1.call-start
  7.3 0.8 copy.18
  8.1 0.1 eq.40
  8.3 0.1 reshape.73
  8.4 1.1 reduce-window.6
  9.6 0.2 slice_reduce_fusion
  9.8 0.1 fusion.10
  9.9 0.0 copy-start
  9.9 0.6 copy-done
  10.5 0.3 fusion.8
  10.8 0.3 select_reduce_fusion
  11.1 20.2 %all-gather.2.cloned.1.call-done = bf16[256,3072]{1,0:T(8,128)(2,1)} async-done(((bf16[256,768]{1,0:T(8,128)(2,1)}), bf16[256,3072]{1,0:T(8,128)(2,1)}) %all-gather.2.cloned.1.call-update) | async-done | bytes 1572880 | tf_op jit(solution)/shard_map/all_gather | solution.py:32
  31.3 13.8 %gather_fusion = bf16[1024,3072]{1,0:T(8,128)(2,1)} fusion(bf16[256,3072]{1,0:T(8,128)(2,1)} %all-gather.2.cloned.1.call-done, s32[1024]{0:T(1024)S(1)} %broadcast_clamp_fusion), kind=kCustom, calls=%fused_computation | custom fusion | bytes 12587008 | tf_op jit(solution)/shard_map/gather | solution.py:33
  45.2 3.3 broadcast_select_fusion
  48.4 143.9 %all_to_all.10 = bf16[8,128,3072]{2,1,0:T(8,128)(2,1)} all-to-all(bf16[8,128,3072]{2,1,0:T(8,128)(2,1)S(1)} %broadcast_select_fusion), channel_id=1, replica_groups=mesh['ep'=8,'tp'=4] {'ep'}, dimensions={0} | all-to-all | bytes 12582912 | tf_op jit(solution)/shard_map/all_to_all | solution.py:35
  192.3 37.9 %fusion.4 = bf16[1024,3072]{1,0:T(8,128)(2,1)} fusion(bf16[1,2048,3072]{2,1,0:T(8,128)(2,1)} %param.9, bf16[1024,3072]{1,0:T(8,128)(2,1)} %bitcast.35, bf16[1,3072,2048]{2,1,0:T(8,128)(2,1)} %param.8), kind=kOutput, calls=%fused_computation.9 | convolution fusion | flops 25783435264 | bytes 37748736 | tf_op jit(solution)/shard_map/dot_general | solution.py:39
  230.2 0.0 copy-start.1
  230.2 0.0 copy-start.2
  230.2 0.0 copy-start.3
  230.2 0.0 reduce-scatter.2.cloned.1.call-update
  230.2 56.6 %reduce-scatter.2.cloned.1.call-done = bf16[1024,768]{1,0:T(8,128)(2,1)} async-done(((bf16[1024,3072]{1,0:T(8,128)(2,1)}), bf16[1024,768]{1,0:T(8,128)(2,1)}) %reduce-scatter.2.cloned.1.call-update) | async-done | bytes 1572880 | tf_op jit(solution)/shard_map/reduce_scatter | solution.py:40
  286.9 5.5 %all-to-all-start.1 = ((bf16[8,128,768]{2,1,0:T(8,128)(2,1)}), bf16[8,128,768]{2,1,0:T(8,128)(2,1)S(1)}, u32[]{:S(2)}, u32[]{:S(2)}) async-start(bf16[8,128,768]{2,1,0:T(8,128)(2,1)} %bitcast.36), calls=%async_computation.2 | async-start | bytes 3145728 | tf_op jit(solution)/shard_map/all_to_all | solution.py:44
  292.4 0.0 copy-done.1
  292.4 0.1 reduce_sum.25
  292.5 0.1 copy.20
  292.6 0.0 copy-done.2
  292.6 0.0 copy-done.3
  292.7 36.7 %all-to-all-done.1 = bf16[8,128,768]{2,1,0:T(8,128)(2,1)S(1)} async-done(((bf16[8,128,768]{2,1,0:T(8,128)(2,1)}), bf16[8,128,768]{2,1,0:T(8,128)(2,1)S(1)}, u32[]{:S(2)}, u32[]{:S(2)}) %all-to-all-start.1) | async-done | bytes 1572896 | tf_op jit(solution)/shard_map/all_to_all | solution.py:44
  329.4 1.2 gather_fusion.1
  330.6 1.2 gather_fusion.2
  331.7 1.0 add_convert_fusion
  (11 shorter events, 0.1 us)
Async XLA Ops:
  6.5 24.8 %all-gather.2.cloned.1.call-start = ((), (), s32[]{:S(2)}) async-start(), calls=%async_computation.3 | async-start | bytes 1966080 | tf_op jit(solution)/shard_map/all_gather | solution.py:32
  7.3 279.6 %reduce-scatter.2.cloned.1.call-start = ((), (), s32[]{:S(2)}) async-start(), calls=%async_computation.4 | async-start | bytes 7864320 | tf_op jit(solution)/shard_map/reduce_scatter | solution.py:40
  9.9 0.6 copy-start
  230.2 62.2 %copy-start.1 = (s32[512]{0:T(512)S(1)}, s32[512]{0:T(512)}, u32[]{:S(2)}) copy-start(s32[512]{0:T(512)} %copy-done) | copy-start | bytes 6148
  230.2 62.4 %copy-start.2 = (s32[256,2]{0,1:T(2,128)S(1)}, s32[256,2]{0,1:T(2,128)}, u32[]{:S(2)}) copy-start(s32[256,2]{0,1:T(2,128)} %param.6) | copy-start | bytes 6148
  230.2 62.5 %copy-start.3 = (f32[256,2]{0,1:T(2,128)S(1)}, f32[256,2]{0,1:T(2,128)}, u32[]{:S(2)}) copy-start(f32[256,2]{0,1:T(2,128)} %param.7) | copy-start | bytes 6148
  286.9 42.5 %all-to-all-start.1 = ((bf16[8,128,768]{2,1,0:T(8,128)(2,1)}), bf16[8,128,768]{2,1,0:T(8,128)(2,1)S(1)}, u32[]{:S(2)}, u32[]{:S(2)}) async-start(bf16[8,128,768]{2,1,0:T(8,128)(2,1)} %bitcast.36), calls=%async_computation.2 | async-start | bytes 3145728 | tf_op jit(solution)/shard_map/all_to_all | solution.py:44
Sparse Core Ops, SparseCore 0:
  8.9 22.3 all-gather.1
  230.3 56.4 reduce-scatter.1
where the time goes:
time: 340 us
  blocking collectives  144 us (42%)
  waiting for transfers between devices  114 us (34%)
  matrix products  37.9 us (11%)
  local copies, waits for them, and re-layouts  18.3 us (5%)
  between operations  13.5 us (4%)
  other arithmetic  6.14 us (2%)
  starting transfers between devices  5.55 us (2%)
    all_to_all x1, blocking collectives, per_device(): lax.all_to_all(outgoing, 'ep', split_axis=0, concat_axis=0, tiled=True)  144 us
    reduce_scatter x1, waiting for transfers between devices, per_device(): lax.psum_scatter(partial_value.astype(jnp.bfloat16), 'tp', scatter_dimens...  56.6 us
    dot_general x1, matrix products, per_device(): jnp.dot(hidden, down_matrix, preferred_element_type=jnp.float32)  37.9 us
    all_to_all x1, waiting for transfers between devices, per_device(): lax.all_to_all(result, 'ep', split_axis=0, concat_axis=0, tiled=True)  36.7 us
    all_gather x1, waiting for transfers between devices, per_device(): portion = lax.all_gather(tokens, 'tp', axis=1, tiled=True)  20.2 us
    gather x1, local copies, waits for them, and re-layouts, per_device(): portion[source]  13.8 us
  transfers between devices with their start and end apart: 3, of which 3 were waited for; matrix products, arithmetic and copies ran while one was open for 1% of the time, Pallas kernels for 0%

commit v1 on v0

v1 whole, which is shorter than its diff:
```python
import functools

import jax
import jax.numpy as jnp
from jax import lax
from jax.experimental import pallas as pl
from jax.experimental.pallas import tpu as pltpu
from jax.sharding import PartitionSpec as P

BF16 = jnp.bfloat16
F32 = jnp.float32


def pick_kernel(places, me, slot, routes_ref, tokens_ref, target_ref, *row_refs):
    count = routes_ref.shape[0]
    first, second = routes_ref[:, 0:1], routes_ref[:, 1:2]
    expert = lax.broadcasted_iota(jnp.int32, (count, 128), 1)
    is_first, is_second = expert == first, expert == second
    member = (is_first | is_second).astype(F32).astype(BF16)
    earlier = (
        lax.broadcasted_iota(jnp.int32, (count, count), 1) < lax.broadcasted_iota(jnp.int32, (count, count), 0)
    ).astype(F32).astype(BF16)
    before = jnp.dot(earlier, member, preferred_element_type=F32).astype(jnp.int32)
    index = me[0]
    high = (expert >> 1) - (index >> 1)
    place = jnp.where(high < 0, high + places // 2, high) * 2 + ((expert + index) & 1)
    spot = place * slot + before
    target_first = jnp.sum(jnp.where(is_first, spot, 0), axis=1, keepdims=True)
    target_second = jnp.sum(jnp.where(is_second, spot, 0), axis=1, keepdims=True)
    target_ref[:, 0:1] = target_first
    target_ref[:, 1:2] = target_second
    tokens = tokens_ref[...]
    for r in range(places):
        lane = lax.broadcasted_iota(jnp.int32, (count, slot), 1) + r * slot
        chosen = ((lane == target_first) | (lane == target_second)).astype(F32).astype(BF16)
        rows = lax.dot_general(chosen, tokens, (((0,), (0,)), ((), ())), preferred_element_type=F32)
        row_refs[r][...] = rows.astype(BF16)


def pick_rows(routes, tokens, me, slot, places):
    count, width = tokens.shape
    vmem = pl.BlockSpec(memory_space=pltpu.VMEM)

    def body(me_ref, *refs):
        pick_kernel(places, me_ref, slot, *refs)

    return pl.pallas_call(
        body,
        in_specs=[pl.BlockSpec(memory_space=pltpu.SMEM), vmem, vmem],
        out_specs=[vmem] * (places + 1),
        out_shape=[jax.ShapeDtypeStruct((count, 2), jnp.int32)]
        + [jax.ShapeDtypeStruct((slot, width), BF16)] * places,
        compiler_params=pltpu.CompilerParams(vmem_limit_bytes=32 << 20),
        cost_estimate=pl.CostEstimate(flops=2 * count * slot * places * width, bytes_accessed=4 << 20, transcendentals=0),
        name="pick_rows",
    )(me, routes, tokens)


def combine_rows(target, gates, returned, slot):
    count = target.shape[0]
    width = returned[0].shape[1]
    vmem = pl.BlockSpec(memory_space=pltpu.VMEM)

    def body(target_ref, gates_ref, *refs):
        out_ref = refs[-1]
        total = None
        for k in range(2):
            picked = None
            for r, rows_ref in enumerate(refs[:-1]):
                lane = lax.broadcasted_iota(jnp.int32, (count, slot), 1) + r * slot
                chosen = (lane == target_ref[:, k : k + 1]).astype(F32).astype(BF16)
                part = jnp.dot(chosen, rows_ref[...], preferred_element_type=F32)
                picked = part if picked is None else picked + part
            weighted = gates_ref[:, k : k + 1] * picked
            total = weighted if total is None else total + weighted
        out_ref[...] = total.astype(BF16)

    return pl.pallas_call(
        body,
        in_specs=[vmem] * (2 + len(returned)),
        out_specs=vmem,
        out_shape=jax.ShapeDtypeStruct((count, width), BF16),
        compiler_params=pltpu.CompilerParams(vmem_limit_bytes=32 << 20),
        cost_estimate=pl.CostEstimate(
            flops=4 * count * slot * len(returned) * width, bytes_accessed=4 << 20, transcendentals=0
        ),
        name="combine_rows",
    )(target, gates, *returned)


def feed_forward(order, pieces, up, down, hidden_block):
    n = len(pieces)
    rows, width = pieces[0].shape
    hidden, features = down.shape
    steps = hidden // hidden_block
    half = n // 2

    def body(order_ref, *refs):
        piece_refs, up_refs, down_ref = refs[:n], refs[n : 2 * n], refs[2 * n]
        near_refs, far_ref, total = refs[2 * n + 1 : 2 * n + 1 + half], refs[-2], refs[-1]
        step = pl.program_id(0)
        raised = None
        for piece_ref, up_ref in zip(piece_refs, up_refs):
            part = jnp.dot(piece_ref[...], up_ref[...], preferred_element_type=F32)
            raised = part if raised is None else raised + part
        active = (raised / (1.0 + jnp.exp(-raised))).astype(BF16)
        lowered = jnp.dot(active, down_ref[...], preferred_element_type=F32)

        @pl.when(step == 0)
        def _():
            total[...] = lowered

        @pl.when(step > 0)
        def _():
            total[...] += lowered

        @pl.when(step == steps - 1)
        def _():
            for i in range(n):
                start = pl.multiple_of(order_ref[i] * width, 128)
                value = total[:, pl.ds(start, width)].astype(BF16)
                if i < half:
                    near_refs[i][...] = value
                else:
                    far_ref[i - half] = value

    def up_spec(i):
        return pl.BlockSpec((width, hidden_block), lambda s, order_ref: (order_ref[i], s))

    whole = pl.BlockSpec((rows, width), lambda s, order_ref: (0, 0))
    return pl.pallas_call(
        body,
        grid_spec=pltpu.PrefetchScalarGridSpec(
            num_scalar_prefetch=1,
            grid=(steps,),
            in_specs=[whole] * n
            + [up_spec(i) for i in range(n)]
            + [pl.BlockSpec((hidden_block, features), lambda s, order_ref: (s, 0))],
            out_specs=[whole] * half + [pl.BlockSpec((half, rows, width), lambda s, order_ref: (0, 0, 0))],
            scratch_shapes=[pltpu.VMEM((rows, features), F32)],
        ),
        out_shape=[jax.ShapeDtypeStruct((rows, width), BF16)] * half
        + [jax.ShapeDtypeStruct((half, rows, width), BF16)],
        compiler_params=pltpu.CompilerParams(vmem_limit_bytes=48 << 20),
        cost_estimate=pl.CostEstimate(
            flops=4 * rows * hidden * features,
            bytes_accessed=4 * hidden * features + 4 * rows * features,
            transcendentals=rows * hidden,
        ),
        name="feed_forward",
    )(order, *pieces, *([up] * n), down)


def per_device(tokens, routes, route_gates, up_weight, down_weight):
    places, ranks = lax.axis_size("ep"), lax.axis_size("tp")
    count = tokens.shape[0]
    slot = 4 * count // places
    layers, planes = places // 2, ranks // 2
    group = max(1, min(layers, 256 // (2 * slot)))
    up, down = up_weight[0], down_weight[0]
    me, rank = lax.axis_index("ep"), lax.axis_index("tp")

    def ep_hop(value, place, back=False):
        far, flip = place // 2, place % 2
        pairs = [(i, (i // 2 + far) % layers * 2 + (i % 2 ^ flip)) for i in range(places)]
        return lax.ppermute(value, "ep", [(b, a) for a, b in pairs] if back else pairs)

    def plane_hop(value, far):
        return lax.ppermute(value, "tp", [(i, (i // 2 + far) % planes * 2 + i % 2) for i in range(ranks)])

    def core_hop(value):
        return lax.ppermute(value, "tp", [(i, i ^ 1) for i in range(ranks)])

    order = jnp.stack(
        [(rank // 2 - far) % planes * 2 + rank % 2 for far in range(planes)]
        + [(rank // 2 - far) % planes * 2 + (1 - rank % 2) for far in range(planes)]
    ).astype(jnp.int32)
    target, *picked = pick_rows(routes, tokens, me.reshape(1).astype(jnp.int32), slot, places)
    returned = [None] * places
    arrived = [picked[0]] + [ep_hop(picked[place], place) for place in range(1, places)]
    for chunk in range(layers // group):
        members = range(chunk * 2 * group, (chunk + 1) * 2 * group)
        own = jnp.concatenate([arrived[place] for place in members], axis=0)
        same_core = [own] + [plane_hop(own, far) for far in range(1, planes)]
        other_core = [core_hop(piece) for piece in same_core]
        *near, stacked = feed_forward(order, same_core + other_core, up, down, 256)
        crossed = core_hop(stacked)
        summed = near[0].astype(F32) + crossed[0].astype(F32)
        for far in range(1, planes):
            outgoing = (near[far].astype(F32) + crossed[far].astype(F32)).astype(BF16)
            summed = summed + plane_hop(outgoing, planes - far).astype(F32)
        for i, place in enumerate(members):
            result = summed[i * slot : (i + 1) * slot].astype(BF16)
            returned[place] = result if place == 0 else ep_hop(result, place, back=True)
    return combine_rows(target, route_gates, returned, slot)


def solution(mesh):
    in_specs = (
        P("ep", "tp"),
        P("ep", None),
        P("ep", None),
        P("ep", None, "tp"),
        P("ep", "tp", None),
    )
    out_specs = P("ep", "tp")
    return jax.shard_map(
        per_device, mesh=mesh, in_specs=in_specs, out_specs=out_specs, check_vma=False
    )
```

time: 340 us -> 189 us (0.56)
  blocking collectives: 144 us -> 0 us
  Pallas kernels: 0 us -> 84.4 us
  waiting for transfers between devices: 114 us -> 63.5 us
  matrix products: 37.9 us -> 0 us
  starting transfers between devices: 5.55 us -> 37.2 us
  local copies, waits for them, and re-layouts: 18.3 us -> 2.16 us
  between operations: 13.5 us -> 0.28 us
  other arithmetic: 6.14 us -> 1.09 us
    all_to_all x1 -> x0, blocking collectives: 144 us -> none  [per_device(): lax.all_to_all(outgoing, 'ep', split_axis=0, concat_axis=0, tiled=True)]
    pallas_call x0 -> x6, Pallas kernels: none -> 84.4 us  [the longest x4 80.7 us: feed_forward(): pl.pallas_call(body, grid_spec=pltpu.PrefetchScalarGridSpec(num_scalar_pr...]
    ppermute x0 -> x34, waiting for transfers between devices: none -> 63.5 us  [the longest x14 32.4 us: ep_hop(): lax.ppermute(value, 'ep', [(b, a) for a, b in pairs] if back else pairs)]
    reduce_scatter x1 -> x0, waiting for transfers between devices: 56.6 us -> none  [per_device(): lax.psum_scatter(partial_value.astype(jnp.bfloat16), 'tp', scatter_dimens...]
    dot_general x1 -> x0, matrix products: 37.9 us -> none  [per_device(): jnp.dot(hidden, down_matrix, preferred_element_type=jnp.float32)]
    ppermute x0 -> x34, starting transfers between devices: none -> 37.2 us  [the longest x14 21 us: ep_hop(): lax.ppermute(value, 'ep', [(b, a) for a, b in pairs] if back else pairs)]
    all_to_all x1 -> x0, waiting for transfers between devices: 36.7 us -> none  [per_device(): lax.all_to_all(result, 'ep', split_axis=0, concat_axis=0, tiled=True)]
    all_gather x1 -> x0, waiting for transfers between devices: 20.2 us -> none  [per_device(): portion = lax.all_gather(tokens, 'tp', axis=1, tiled=True)]
  transfers between devices with their start and end apart: 3 -> 34, of which waited for: 3 -> 11; matrix products, arithmetic and copies ran while one was open for 1% -> 1% of each run, Pallas kernels for 0% -> 43%
where the time goes in v1:
time: 189 us
  Pallas kernels  84.4 us (45%)
  waiting for transfers between devices  63.5 us (34%)
  starting transfers between devices  37.2 us (20%)
  local copies, waits for them, and re-layouts  2.16 us (1%)
    pallas_call x4, Pallas kernels, feed_forward(): pl.pallas_call(body, grid_spec=pltpu.PrefetchScalarGridSpec(num_scalar_pr...  80.7 us
    ppermute x14, waiting for transfers between devices, ep_hop(): lax.ppermute(value, 'ep', [(b, a) for a, b in pairs] if back else pairs)  32.4 us
    ppermute x8, waiting for transfers between devices, plane_hop(): lax.ppermute(value, 'tp', [(i, (i // 2 + far) % planes * 2 + i % 2) for i...  31.1 us
    ppermute x14, starting transfers between devices, ep_hop(): lax.ppermute(value, 'ep', [(b, a) for a, b in pairs] if back else pairs)  21 us
    ppermute x8, starting transfers between devices, plane_hop(): lax.ppermute(value, 'tp', [(i, (i // 2 + far) % planes * 2 + i % 2) for i...  13.5 us
  transfers between devices with their start and end apart: 34, of which 11 were waited for; matrix products, arithmetic and copies ran while one was open for 1% of the time, Pallas kernels for 43%

profile of v1, /device:TPU:0, one launch (start us, length us, event | category | flops | bytes accessed | tf_op | source)
XLA Modules:
  0.0 188.7 jit_solution(13440357094777689485)
XLA Ops:
  0.0 0.8 copy.6.refs_0_
  0.8 1.0 copy-done
  1.8 1.1 pick_rows.1
  3.0 5.1 %collective-permute-start.25 = (bf16[128,768]{1,0:T(8,128)(2,1)S(1)}, bf16[128,768]{1,0:T(8,128)(2,1)S(1)}, u32[]{:S(2)}, u32[]{:S(2)}) collective-permute-start(bf16[128,768]{1,0:T(8,128)(2,1)S(1)} %get-tuple-element.42), channel_id=1, source_target_pairs={{0,24},{4,28},{8,0},{12,4},{16,8},{20,12},{24,16},{28,20},{1,25},{... | collective-permute-start | bytes 589832 | tf_op jit(solution)/shard_map/ppermute | solution.py:166
  8.1 1.4 collective-permute-start.26
  9.5 4.0 %collective-permute-done.25 = bf16[128,768]{1,0:T(8,128)(2,1)S(1)} collective-permute-done((bf16[128,768]{1,0:T(8,128)(2,1)S(1)}, bf16[128,768]{1,0:T(8,128)(2,1)S(1)}, u32[]{:S(2)}, u32[]{:S(2)}) %collective-permute-start.25) | collective-permute-done | bytes 196640 | tf_op jit(solution)/shard_map/ppermute | solution.py:166
  13.4 4.2 %collective-permute-done.26 = bf16[128,768]{1,0:T(8,128)(2,1)S(1)} collective-permute-done((bf16[128,768]{1,0:T(8,128)(2,1)S(1)}, bf16[128,768]{1,0:T(8,128)(2,1)S(1)}, u32[]{:S(2)}, u32[]{:S(2)}) %collective-permute-start.26) | collective-permute-done | bytes 196640 | tf_op jit(solution)/shard_map/ppermute | solution.py:166
  17.7 1.6 collective-permute-start.27
  19.2 2.3 %collective-permute-start.17 = (bf16[128,768]{1,0:T(8,128)(2,1)S(1)}, bf16[128,768]{1,0:T(8,128)(2,1)S(1)}, u32[]{:S(2)}, u32[]{:S(2)}) collective-permute-start(bf16[128,768]{1,0:T(8,128)(2,1)S(1)} %get-tuple-element.38), channel_id=1, source_target_pairs={{0,20},{4,16},{8,28},{12,24},{16,4},{20,0},{24,12},{28,8},{1,21},{... | collective-permute-start | bytes 589832 | tf_op jit(solution)/shard_map/ppermute | solution.py:166
  21.6 9.5 %collective-permute-start.7 = (bf16[128,768]{1,0:T(8,128)(2,1)S(1)}, bf16[128,768]{1,0:T(8,128)(2,1)S(1)}, u32[]{:S(2)}, u32[]{:S(2)}) collective-permute-start(bf16[128,768]{1,0:T(8,128)(2,1)S(1)} %get-tuple-element.32), channel_id=1, source_target_pairs={{0,8},{4,12},{8,16},{12,20},{16,24},{20,28},{24,0},{28,4},{1,9},{5... | collective-permute-start | bytes 589832 | tf_op jit(solution)/shard_map/ppermute | solution.py:166
  31.1 7.4 %collective-permute-done.16 = bf16[128,768]{1,0:T(8,128)(2,1)S(1)} collective-permute-done((bf16[128,768]{1,0:T(8,128)(2,1)S(1)}, bf16[128,768]{1,0:T(8,128)(2,1)S(1)}, u32[]{:S(2)}, u32[]{:S(2)}) %collective-permute-start.16) | collective-permute-done | bytes 196640 | tf_op jit(solution)/shard_map/ppermute | solution.py:166
  38.6 5.5 %collective-permute-start.18 = (bf16[256,768]{1,0:T(8,128)(2,1)S(1)}, bf16[256,768]{1,0:T(8,128)(2,1)S(1)}, u32[]{:S(2)}, u32[]{:S(2)}) collective-permute-start(bf16[256,768]{1,0:T(8,128)(2,1)S(1)} %constant_dynamic-update-slice_fusion.4.refs_0_), channel_id=1, source_target_pairs={{0,2},{1,3},{2,0},{3,1},{4,6},{5,7},{6,4},{7,5},{8,10},{9,11},{10,... | collective-permute-start | bytes 1179656 | tf_op jit(solution)/shard_map/ppermute | solution.py:169
  44.2 0.5 collective-permute-start
  44.8 0.3 collective-permute-start.19
  45.1 6.4 %collective-permute-done = bf16[128,768]{1,0:T(8,128)(2,1)S(1)} collective-permute-done((bf16[128,768]{1,0:T(8,128)(2,1)S(1)}, bf16[128,768]{1,0:T(8,128)(2,1)S(1)}, u32[]{:S(2)}, u32[]{:S(2)}) %collective-permute-start) | collective-permute-done | bytes 196640 | tf_op jit(solution)/shard_map/ppermute | solution.py:166
  51.8 2.0 %collective-permute-start.1 = (bf16[256,768]{1,0:T(8,128)(2,1)S(1)}, bf16[256,768]{1,0:T(8,128)(2,1)S(1)}, u32[]{:S(2)}, u32[]{:S(2)}) collective-permute-start(bf16[256,768]{1,0:T(8,128)(2,1)S(1)} %constant_dynamic-update-slice_fusion.refs_0_), channel_id=1, source_target_pairs={{0,2},{1,3},{2,0},{3,1},{4,6},{5,7},{6,4},{7,5},{8,10},{9,11},{10,... | collective-permute-start | bytes 1179656 | tf_op jit(solution)/shard_map/ppermute | solution.py:169
  53.8 0.2 collective-permute-start.20
  53.9 20.2 %feed_forward.7 = (bf16[256,768]{1,0:T(8,128)(2,1)S(1)}, bf16[256,768]{1,0:T(8,128)(2,1)S(1)}, bf16[2,256,768]{2,1,0:T(8,128)(2,1)S(1)}) custom-call(s32[4]{0:T(128)S(1)} %pad_add_fusion.order_ref, bf16[256,768]{1,0:T(8,128)(2,1)S(1)} %constant_dynamic-update-slice_fusion.6.refs_0_, bf16[256,768]{1,0:T(8,128)(2,1)S(1)} %collective-permute-done.27.refs_1_, ...), custom_call_target="tpu_custom_call" | custom-call | flops 6442450944 | bytes 28311552 | tf_op jit(solution)/shard_map/feed_forward/pallas_call | solution.py:131
  74.1 0.4 collective-permute-start.2
  74.5 0.2 collective-permute-start.11
  74.7 0.4 collective-permute-start.3
  75.1 0.2 collective-permute-start.30
  75.2 20.2 %feed_forward.6 = (bf16[256,768]{1,0:T(8,128)(2,1)S(1)}, bf16[256,768]{1,0:T(8,128)(2,1)S(1)}, bf16[2,256,768]{2,1,0:T(8,128)(2,1)S(1)}) custom-call(s32[4]{0:T(128)S(1)} %pad_add_fusion.order_ref, bf16[256,768]{1,0:T(8,128)(2,1)S(1)} %constant_dynamic-update-slice_fusion.4.refs_0_, bf16[256,768]{1,0:T(8,128)(2,1)S(1)} %collective-permute-done.18.refs_1_, ...), custom_call_target="tpu_custom_call" | custom-call | flops 6442450944 | bytes 28311552 | tf_op jit(solution)/shard_map/feed_forward/pallas_call | solution.py:131
  95.4 0.4 collective-permute-start.21
  95.8 20.2 %feed_forward.5 = (bf16[256,768]{1,0:T(8,128)(2,1)S(1)}, bf16[256,768]{1,0:T(8,128)(2,1)S(1)}, bf16[2,256,768]{2,1,0:T(8,128)(2,1)S(1)}) custom-call(s32[4]{0:T(128)S(1)} %pad_add_fusion.order_ref, bf16[256,768]{1,0:T(8,128)(2,1)S(1)} %constant_dynamic-update-slice_fusion.2.refs_0_, bf16[256,768]{1,0:T(8,128)(2,1)S(1)} %collective-permute-done.9.refs_1_, ...), custom_call_target="tpu_custom_call" | custom-call | flops 6442450944 | bytes 28311552 | tf_op jit(solution)/shard_map/feed_forward/pallas_call | solution.py:131
  116.0 0.2 collective-permute-start.12
  116.2 20.2 %feed_forward.4 = (bf16[256,768]{1,0:T(8,128)(2,1)S(1)}, bf16[256,768]{1,0:T(8,128)(2,1)S(1)}, bf16[2,256,768]{2,1,0:T(8,128)(2,1)S(1)}) custom-call(s32[4]{0:T(128)S(1)} %pad_add_fusion.order_ref, bf16[256,768]{1,0:T(8,128)(2,1)S(1)} %constant_dynamic-update-slice_fusion.refs_0_, bf16[256,768]{1,0:T(8,128)(2,1)S(1)} %collective-permute-done.1.refs_1_, ...), custom_call_target="tpu_custom_call" | custom-call | flops 6442450944 | bytes 28311552 | tf_op jit(solution)/shard_map/feed_forward/pallas_call | solution.py:131
  136.4 0.4 collective-permute-start.4
  137.0 0.2 collective-permute-start.31
  137.1 0.1 fusion.3
  137.2 2.0 %collective-permute-start.22 = (bf16[256,768]{1,0:T(8,128)(2,1)S(1)}, bf16[256,768]{1,0:T(8,128)(2,1)S(1)}, u32[]{:S(2)}, u32[]{:S(2)}) collective-permute-start(bf16[256,768]{1,0:T(8,128)(2,1)S(1)} %fusion.3), channel_id=1, source_target_pairs={{0,2},{1,3},{2,0},{3,1},{4,6},{5,7},{6,4},{7,5},{8,10},{9,11},{10,... | collective-permute-start | bytes 1179656 | tf_op jit(solution)/shard_map/ppermute | solution.py:169
  139.3 0.2 collective-permute-start.13
  139.6 2.0 %collective-permute-start.5 = (bf16[256,768]{1,0:T(8,128)(2,1)S(1)}, bf16[256,768]{1,0:T(8,128)(2,1)S(1)}, u32[]{:S(2)}, u32[]{:S(2)}) collective-permute-start(bf16[256,768]{1,0:T(8,128)(2,1)S(1)} %fusion.9), channel_id=1, source_target_pairs={{0,2},{1,3},{2,0},{3,1},{4,6},{5,7},{6,4},{7,5},{8,10},{9,11},{10,... | collective-permute-start | bytes 1179656 | tf_op jit(solution)/shard_map/ppermute | solution.py:169
  141.6 7.4 %collective-permute-done.31 = bf16[256,768]{1,0:T(8,128)(2,1)S(1)} collective-permute-done((bf16[256,768]{1,0:T(8,128)(2,1)S(1)}, bf16[256,768]{1,0:T(8,128)(2,1)S(1)}, u32[]{:S(2)}, u32[]{:S(2)}) %collective-permute-start.31) | collective-permute-done | bytes 393248 | tf_op jit(solution)/shard_map/ppermute | solution.py:169
  149.0 0.2 fusion.2
  149.3 8.1 %collective-permute-done.22 = bf16[256,768]{1,0:T(8,128)(2,1)S(1)} collective-permute-done((bf16[256,768]{1,0:T(8,128)(2,1)S(1)}, bf16[256,768]{1,0:T(8,128)(2,1)S(1)}, u32[]{:S(2)}, u32[]{:S(2)}) %collective-permute-start.22) | collective-permute-done | bytes 393248 | tf_op jit(solution)/shard_map/ppermute | solution.py:169
  157.4 0.2 fusion.5
  157.7 8.2 %collective-permute-done.13 = bf16[256,768]{1,0:T(8,128)(2,1)S(1)} collective-permute-done((bf16[256,768]{1,0:T(8,128)(2,1)S(1)}, bf16[256,768]{1,0:T(8,128)(2,1)S(1)}, u32[]{:S(2)}, u32[]{:S(2)}) %collective-permute-start.13) | collective-permute-done | bytes 393248 | tf_op jit(solution)/shard_map/ppermute | solution.py:169
  165.8 0.2 fusion.8
  166.0 7.4 %collective-permute-done.5 = bf16[256,768]{1,0:T(8,128)(2,1)S(1)} collective-permute-done((bf16[256,768]{1,0:T(8,128)(2,1)S(1)}, bf16[256,768]{1,0:T(8,128)(2,1)S(1)}, u32[]{:S(2)}, u32[]{:S(2)}) %collective-permute-start.5) | collective-permute-done | bytes 393248 | tf_op jit(solution)/shard_map/ppermute | solution.py:169
  173.5 0.1 fusion.11
  173.7 1.1 collective-permute-start.15
  174.7 0.8 collective-permute-start.6
  175.6 0.1 copy.7.gates_ref
  175.7 2.1 %collective-permute-done.24.refs_5_ = bf16[128,768]{1,0:T(8,128)(2,1)S(1)} collective-permute-done((bf16[128,768]{1,0:T(8,128)(2,1)S(1)}, bf16[128,768]{1,0:T(8,128)(2,1)S(1)}, u32[]{:S(2)}, u32[]{:S(2)}) %collective-permute-start.24) | collective-permute-done | bytes 196640 | tf_op jit(solution)/shard_map/ppermute | solution.py:166
  177.8 4.0 %collective-permute-done.14.refs_2_ = bf16[128,768]{1,0:T(8,128)(2,1)S(1)} collective-permute-done((bf16[128,768]{1,0:T(8,128)(2,1)S(1)}, bf16[128,768]{1,0:T(8,128)(2,1)S(1)}, u32[]{:S(2)}, u32[]{:S(2)}) %collective-permute-start.14) | collective-permute-done | bytes 196640 | tf_op jit(solution)/shard_map/ppermute | solution.py:166
  181.8 4.3 %collective-permute-done.15.refs_3_ = bf16[128,768]{1,0:T(8,128)(2,1)S(1)} collective-permute-done((bf16[128,768]{1,0:T(8,128)(2,1)S(1)}, bf16[128,768]{1,0:T(8,128)(2,1)S(1)}, u32[]{:S(2)}, u32[]{:S(2)}) %collective-permute-start.15) | collective-permute-done | bytes 196640 | tf_op jit(solution)/shard_map/ppermute | solution.py:166
  186.1 2.6 %combine_rows.1 = bf16[256,768]{1,0:T(8,128)(2,1)} custom-call(s32[256,2]{1,0:T(8,128)S(1)} %get-tuple-element.26.target_ref, f32[256,2]{1,0:T(8,128)S(1)} %copy.7.gates_ref, bf16[128,768]{1,0:T(8,128)(2,1)S(1)} %get-tuple-element.54.refs_0_, bf16[128,768]{1,0:T(8,128)(2,1)S(1)} %collective-permute-done.6.refs_1_, ...), custom_call_target="tpu_custom_call" | custom-call | flops 805306368 | bytes 4194304 | tf_op jit(solution)/shard_map/combine_rows/pallas_call | solution.py:78
  (53 shorter events, 1.1 us)
Async XLA Ops:
  0.8 1.0 copy-start
  3.0 10.5 %collective-permute-start.25 = (bf16[128,768]{1,0:T(8,128)(2,1)S(1)}, bf16[128,768]{1,0:T(8,128)(2,1)S(1)}, u32[]{:S(2)}, u32[]{:S(2)}) collective-permute-start(bf16[128,768]{1,0:T(8,128)(2,1)S(1)} %get-tuple-element.42), channel_id=1, source_target_pairs={{0,24},{4,28},{8,0},{12,4},{16,8},{20,12},{24,16},{28,20},{1,25},{... | collective-permute-start | bytes 589832 | tf_op jit(solution)/shard_map/ppermute | solution.py:166
  8.1 9.6 %collective-permute-start.26 = (bf16[128,768]{1,0:T(8,128)(2,1)S(1)}, bf16[128,768]{1,0:T(8,128)(2,1)S(1)}, u32[]{:S(2)}, u32[]{:S(2)}) collective-permute-start(bf16[128,768]{1,0:T(8,128)(2,1)S(1)} %get-tuple-element.43), channel_id=1, source_target_pairs={{0,28},{4,24},{8,4},{12,0},{16,12},{20,8},{24,20},{28,16},{1,29},{... | collective-permute-start | bytes 589832 | tf_op jit(solution)/shard_map/ppermute | solution.py:166
  9.5 29.1 %collective-permute-start.16 = (bf16[128,768]{1,0:T(8,128)(2,1)S(1)}, bf16[128,768]{1,0:T(8,128)(2,1)S(1)}, u32[]{:S(2)}, u32[]{:S(2)}) collective-permute-start(bf16[128,768]{1,0:T(8,128)(2,1)S(1)} %get-tuple-element.37), channel_id=1, source_target_pairs={{0,16},{4,20},{8,24},{12,28},{16,0},{20,4},{24,8},{28,12},{1,17},{... | collective-permute-start | bytes 589832 | tf_op jit(solution)/shard_map/ppermute | solution.py:166
  17.7 26.5 %collective-permute-start.27 = (bf16[256,768]{1,0:T(8,128)(2,1)S(1)}, bf16[256,768]{1,0:T(8,128)(2,1)S(1)}, u32[]{:S(2)}, u32[]{:S(2)}) collective-permute-start(bf16[256,768]{1,0:T(8,128)(2,1)S(1)} %constant_dynamic-update-slice_fusion.6.refs_0_), channel_id=1, source_target_pairs={{0,2},{1,3},{2,0},{3,1},{4,6},{5,7},{6,4},{7,5},{8,10},{9,11},{10,... | collective-permute-start | bytes 1179656 | tf_op jit(solution)/shard_map/ppermute | solution.py:169
  19.2 19.3 %collective-permute-start.17 = (bf16[128,768]{1,0:T(8,128)(2,1)S(1)}, bf16[128,768]{1,0:T(8,128)(2,1)S(1)}, u32[]{:S(2)}, u32[]{:S(2)}) collective-permute-start(bf16[128,768]{1,0:T(8,128)(2,1)S(1)} %get-tuple-element.38), channel_id=1, source_target_pairs={{0,20},{4,16},{8,28},{12,24},{16,4},{20,0},{24,12},{28,8},{1,21},{... | collective-permute-start | bytes 589832 | tf_op jit(solution)/shard_map/ppermute | solution.py:166
  21.6 22.7 %collective-permute-start.7 = (bf16[128,768]{1,0:T(8,128)(2,1)S(1)}, bf16[128,768]{1,0:T(8,128)(2,1)S(1)}, u32[]{:S(2)}, u32[]{:S(2)}) collective-permute-start(bf16[128,768]{1,0:T(8,128)(2,1)S(1)} %get-tuple-element.32), channel_id=1, source_target_pairs={{0,8},{4,12},{8,16},{12,20},{16,24},{20,28},{24,0},{28,4},{1,9},{5... | collective-permute-start | bytes 589832 | tf_op jit(solution)/shard_map/ppermute | solution.py:166
  31.1 13.7 %collective-permute-start.8 = (bf16[128,768]{1,0:T(8,128)(2,1)S(1)}, bf16[128,768]{1,0:T(8,128)(2,1)S(1)}, u32[]{:S(2)}, u32[]{:S(2)}) collective-permute-start(bf16[128,768]{1,0:T(8,128)(2,1)S(1)} %get-tuple-element.33), channel_id=1, source_target_pairs={{0,12},{4,8},{8,20},{12,16},{16,28},{20,24},{24,4},{28,0},{1,13},{... | collective-permute-start | bytes 589832 | tf_op jit(solution)/shard_map/ppermute | solution.py:166
  38.6 13.1 %collective-permute-start.28 = (bf16[256,768]{1,0:T(8,128)(2,1)S(1)}, bf16[256,768]{1,0:T(8,128)(2,1)S(1)}, u32[]{:S(2)}, u32[]{:S(2)}) collective-permute-start(bf16[256,768]{1,0:T(8,128)(2,1)S(1)} %constant_dynamic-update-slice_fusion.6.refs_0_), channel_id=1, source_target_pairs={{0,1},{1,0},{2,3},{3,2},{4,5},{5,4},{6,7},{7,6},{8,9},{9,8},{10,11... | collective-permute-start | bytes 1179656 | tf_op jit(solution)/shard_map/ppermute | solution.py:172
  38.6 13.1 %collective-permute-start.18 = (bf16[256,768]{1,0:T(8,128)(2,1)S(1)}, bf16[256,768]{1,0:T(8,128)(2,1)S(1)}, u32[]{:S(2)}, u32[]{:S(2)}) collective-permute-start(bf16[256,768]{1,0:T(8,128)(2,1)S(1)} %constant_dynamic-update-slice_fusion.4.refs_0_), channel_id=1, source_target_pairs={{0,2},{1,3},{2,0},{3,1},{4,6},{5,7},{6,4},{7,5},{8,10},{9,11},{10,... | collective-permute-start | bytes 1179656 | tf_op jit(solution)/shard_map/ppermute | solution.py:169
  44.2 9.6 %collective-permute-start.29 = (bf16[256,768]{1,0:T(8,128)(2,1)S(1)}, bf16[256,768]{1,0:T(8,128)(2,1)S(1)}, u32[]{:S(2)}, u32[]{:S(2)}) collective-permute-start(bf16[256,768]{1,0:T(8,128)(2,1)S(1)} %collective-permute-done.27.refs_1_), channel_id=1, source_target_pairs={{0,1},{1,0},{2,3},{3,2},{4,5},{5,4},{6,7},{7,6},{8,9},{9,8},{10,11... | collective-permute-start | bytes 1179656 | tf_op jit(solution)/shard_map/ppermute | solution.py:172
  44.2 7.3 %collective-permute-start = (bf16[128,768]{1,0:T(8,128)(2,1)S(1)}, bf16[128,768]{1,0:T(8,128)(2,1)S(1)}, u32[]{:S(2)}, u32[]{:S(2)}) collective-permute-start(bf16[128,768]{1,0:T(8,128)(2,1)S(1)} %get-tuple-element.28), channel_id=1, source_target_pairs={{0,4},{4,0},{8,12},{12,8},{16,20},{20,16},{24,28},{28,24},{1,5},{5... | collective-permute-start | bytes 589832 | tf_op jit(solution)/shard_map/ppermute | solution.py:166
  44.8 29.3 %collective-permute-start.19 = (bf16[256,768]{1,0:T(8,128)(2,1)S(1)}, bf16[256,768]{1,0:T(8,128)(2,1)S(1)}, u32[]{:S(2)}, u32[]{:S(2)}) collective-permute-start(bf16[256,768]{1,0:T(8,128)(2,1)S(1)} %constant_dynamic-update-slice_fusion.4.refs_0_), channel_id=1, source_target_pairs={{0,1},{1,0},{2,3},{3,2},{4,5},{5,4},{6,7},{7,6},{8,9},{9,8},{10,11... | collective-permute-start | bytes 1179656 | tf_op jit(solution)/shard_map/ppermute | solution.py:172
  51.6 23.0 %collective-permute-start.9 = (bf16[256,768]{1,0:T(8,128)(2,1)S(1)}, bf16[256,768]{1,0:T(8,128)(2,1)S(1)}, u32[]{:S(2)}, u32[]{:S(2)}) collective-permute-start(bf16[256,768]{1,0:T(8,128)(2,1)S(1)} %constant_dynamic-update-slice_fusion.2.refs_0_), channel_id=1, source_target_pairs={{0,2},{1,3},{2,0},{3,1},{4,6},{5,7},{6,4},{7,5},{8,10},{9,11},{10,... | collective-permute-start | bytes 1179656 | tf_op jit(solution)/shard_map/ppermute | solution.py:169
  51.7 43.7 %collective-permute-start.10 = (bf16[256,768]{1,0:T(8,128)(2,1)S(1)}, bf16[256,768]{1,0:T(8,128)(2,1)S(1)}, u32[]{:S(2)}, u32[]{:S(2)}) collective-permute-start(bf16[256,768]{1,0:T(8,128)(2,1)S(1)} %constant_dynamic-update-slice_fusion.2.refs_0_), channel_id=1, source_target_pairs={{0,1},{1,0},{2,3},{3,2},{4,5},{5,4},{6,7},{7,6},{8,9},{9,8},{10,11... | collective-permute-start | bytes 1179656 | tf_op jit(solution)/shard_map/ppermute | solution.py:172
  51.8 22.9 %collective-permute-start.1 = (bf16[256,768]{1,0:T(8,128)(2,1)S(1)}, bf16[256,768]{1,0:T(8,128)(2,1)S(1)}, u32[]{:S(2)}, u32[]{:S(2)}) collective-permute-start(bf16[256,768]{1,0:T(8,128)(2,1)S(1)} %constant_dynamic-update-slice_fusion.refs_0_), channel_id=1, source_target_pairs={{0,2},{1,3},{2,0},{3,1},{4,6},{5,7},{6,4},{7,5},{8,10},{9,11},{10,... | collective-permute-start | bytes 1179656 | tf_op jit(solution)/shard_map/ppermute | solution.py:169
  53.8 21.3 %collective-permute-start.20 = (bf16[256,768]{1,0:T(8,128)(2,1)S(1)}, bf16[256,768]{1,0:T(8,128)(2,1)S(1)}, u32[]{:S(2)}, u32[]{:S(2)}) collective-permute-start(bf16[256,768]{1,0:T(8,128)(2,1)S(1)} %collective-permute-done.18.refs_1_), channel_id=1, source_target_pairs={{0,1},{1,0},{2,3},{3,2},{4,5},{5,4},{6,7},{7,6},{8,9},{9,8},{10,11... | collective-permute-start | bytes 1179656 | tf_op jit(solution)/shard_map/ppermute | solution.py:172
  74.1 42.1 %collective-permute-start.2 = (bf16[256,768]{1,0:T(8,128)(2,1)S(1)}, bf16[256,768]{1,0:T(8,128)(2,1)S(1)}, u32[]{:S(2)}, u32[]{:S(2)}) collective-permute-start(bf16[256,768]{1,0:T(8,128)(2,1)S(1)} %constant_dynamic-update-slice_fusion.refs_0_), channel_id=1, source_target_pairs={{0,1},{1,0},{2,3},{3,2},{4,5},{5,4},{6,7},{7,6},{8,9},{9,8},{10,11... | collective-permute-start | bytes 1179656 | tf_op jit(solution)/shard_map/ppermute | solution.py:172
  74.5 21.3 %collective-permute-start.11 = (bf16[256,768]{1,0:T(8,128)(2,1)S(1)}, bf16[256,768]{1,0:T(8,128)(2,1)S(1)}, u32[]{:S(2)}, u32[]{:S(2)}) collective-permute-start(bf16[256,768]{1,0:T(8,128)(2,1)S(1)} %collective-permute-done.9.refs_1_), channel_id=1, source_target_pairs={{0,1},{1,0},{2,3},{3,2},{4,5},{5,4},{6,7},{7,6},{8,9},{9,8},{10,11... | collective-permute-start | bytes 1179656 | tf_op jit(solution)/shard_map/ppermute | solution.py:172
  74.7 41.5 %collective-permute-start.3 = (bf16[256,768]{1,0:T(8,128)(2,1)S(1)}, bf16[256,768]{1,0:T(8,128)(2,1)S(1)}, u32[]{:S(2)}, u32[]{:S(2)}) collective-permute-start(bf16[256,768]{1,0:T(8,128)(2,1)S(1)} %collective-permute-done.1.refs_1_), channel_id=1, source_target_pairs={{0,1},{1,0},{2,3},{3,2},{4,5},{5,4},{6,7},{7,6},{8,9},{9,8},{10,11... | collective-permute-start | bytes 1179656 | tf_op jit(solution)/shard_map/ppermute | solution.py:172
  75.1 61.8 %collective-permute-start.30 = (bf16[2,256,768]{2,1,0:T(8,128)(2,1)S(1)}, bf16[2,256,768]{2,1,0:T(8,128)(2,1)S(1)}, u32[]{:S(2)}, u32[]{:S(2)}) collective-permute-start(bf16[2,256,768]{2,1,0:T(8,128)(2,1)S(1)} %get-tuple-element.45), channel_id=1, source_target_pairs={{0,1},{1,0},{2,3},{3,2},{4,5},{5,4},{6,7},{7,6},{8,9},{9,8},{10,11... | collective-permute-start | bytes 2359304 | tf_op jit(solution)/shard_map/ppermute | solution.py:172
  95.4 41.7 %collective-permute-start.21 = (bf16[2,256,768]{2,1,0:T(8,128)(2,1)S(1)}, bf16[2,256,768]{2,1,0:T(8,128)(2,1)S(1)}, u32[]{:S(2)}, u32[]{:S(2)}) collective-permute-start(bf16[2,256,768]{2,1,0:T(8,128)(2,1)S(1)} %get-tuple-element.40), channel_id=1, source_target_pairs={{0,1},{1,0},{2,3},{3,2},{4,5},{5,4},{6,7},{7,6},{8,9},{9,8},{10,11... | collective-permute-start | bytes 2359304 | tf_op jit(solution)/shard_map/ppermute | solution.py:172
  116.0 23.2 %collective-permute-start.12 = (bf16[2,256,768]{2,1,0:T(8,128)(2,1)S(1)}, bf16[2,256,768]{2,1,0:T(8,128)(2,1)S(1)}, u32[]{:S(2)}, u32[]{:S(2)}) collective-permute-start(bf16[2,256,768]{2,1,0:T(8,128)(2,1)S(1)} %get-tuple-element.35), channel_id=1, source_target_pairs={{0,1},{1,0},{2,3},{3,2},{4,5},{5,4},{6,7},{7,6},{8,9},{9,8},{10,11... | collective-permute-start | bytes 2359304 | tf_op jit(solution)/shard_map/ppermute | solution.py:172
  136.4 39.1 %copy-start.1 = (f32[256,2]{0,1:T(2,128)S(1)}, f32[256,2]{0,1:T(2,128)}, u32[]{:S(2)}) copy-start(f32[256,2]{0,1:T(2,128)} %param.7) | copy-start | bytes 6148
  136.4 3.1 %collective-permute-start.4 = (bf16[2,256,768]{2,1,0:T(8,128)(2,1)S(1)}, bf16[2,256,768]{2,1,0:T(8,128)(2,1)S(1)}, u32[]{:S(2)}, u32[]{:S(2)}) collective-permute-start(bf16[2,256,768]{2,1,0:T(8,128)(2,1)S(1)} %get-tuple-element.30), channel_id=1, source_target_pairs={{0,1},{1,0},{2,3},{3,2},{4,5},{5,4},{6,7},{7,6},{8,9},{9,8},{10,11... | collective-permute-start | bytes 2359304 | tf_op jit(solution)/shard_map/ppermute | solution.py:172
  137.0 12.0 %collective-permute-start.31 = (bf16[256,768]{1,0:T(8,128)(2,1)S(1)}, bf16[256,768]{1,0:T(8,128)(2,1)S(1)}, u32[]{:S(2)}, u32[]{:S(2)}) collective-permute-start(bf16[256,768]{1,0:T(8,128)(2,1)S(1)} %fusion), channel_id=1, source_target_pairs={{0,2},{1,3},{2,0},{3,1},{4,6},{5,7},{6,4},{7,5},{8,10},{9,11},{10,... | collective-permute-start | bytes 1179656 | tf_op jit(solution)/shard_map/ppermute | solution.py:169
  137.2 20.2 %collective-permute-start.22 = (bf16[256,768]{1,0:T(8,128)(2,1)S(1)}, bf16[256,768]{1,0:T(8,128)(2,1)S(1)}, u32[]{:S(2)}, u32[]{:S(2)}) collective-permute-start(bf16[256,768]{1,0:T(8,128)(2,1)S(1)} %fusion.3), channel_id=1, source_target_pairs={{0,2},{1,3},{2,0},{3,1},{4,6},{5,7},{6,4},{7,5},{8,10},{9,11},{10,... | collective-permute-start | bytes 1179656 | tf_op jit(solution)/shard_map/ppermute | solution.py:169
  139.3 26.5 %collective-permute-start.13 = (bf16[256,768]{1,0:T(8,128)(2,1)S(1)}, bf16[256,768]{1,0:T(8,128)(2,1)S(1)}, u32[]{:S(2)}, u32[]{:S(2)}) collective-permute-start(bf16[256,768]{1,0:T(8,128)(2,1)S(1)} %fusion.6), channel_id=1, source_target_pairs={{0,2},{1,3},{2,0},{3,1},{4,6},{5,7},{6,4},{7,5},{8,10},{9,11},{10,... | collective-permute-start | bytes 1179656 | tf_op jit(solution)/shard_map/ppermute | solution.py:169
  139.6 33.9 %collective-permute-start.5 = (bf16[256,768]{1,0:T(8,128)(2,1)S(1)}, bf16[256,768]{1,0:T(8,128)(2,1)S(1)}, u32[]{:S(2)}, u32[]{:S(2)}) collective-permute-start(bf16[256,768]{1,0:T(8,128)(2,1)S(1)} %fusion.9), channel_id=1, source_target_pairs={{0,2},{1,3},{2,0},{3,1},{4,6},{5,7},{6,4},{7,5},{8,10},{9,11},{10,... | collective-permute-start | bytes 1179656 | tf_op jit(solution)/shard_map/ppermute | solution.py:169
  149.2 24.5 %collective-permute-start.32 = (bf16[128,768]{1,0:T(8,128)(2,1)S(1)}, bf16[128,768]{1,0:T(8,128)(2,1)S(1)}, u32[]{:S(2)}, u32[]{:S(2)}) collective-permute-start(bf16[128,768]{1,0:T(8,128)(2,1)S(1)} %get-tuple-element.48), channel_id=1, source_target_pairs={{24,0},{28,4},{0,8},{4,12},{8,16},{12,20},{16,24},{20,28},{25,1},{... | collective-permute-start | bytes 589832 | tf_op jit(solution)/shard_map/ppermute | solution.py:166
  149.2 25.5 %collective-permute-start.33 = (bf16[128,768]{1,0:T(8,128)(2,1)S(1)}, bf16[128,768]{1,0:T(8,128)(2,1)S(1)}, u32[]{:S(2)}, u32[]{:S(2)}) collective-permute-start(bf16[128,768]{1,0:T(8,128)(2,1)S(1)} %get-tuple-element.47), channel_id=1, source_target_pairs={{28,0},{24,4},{4,8},{0,12},{12,16},{8,20},{20,24},{16,28},{29,1},{... | collective-permute-start | bytes 589832 | tf_op jit(solution)/shard_map/ppermute | solution.py:166
  157.6 18.1 %collective-permute-start.23 = (bf16[128,768]{1,0:T(8,128)(2,1)S(1)}, bf16[128,768]{1,0:T(8,128)(2,1)S(1)}, u32[]{:S(2)}, u32[]{:S(2)}) collective-permute-start(bf16[128,768]{1,0:T(8,128)(2,1)S(1)} %get-tuple-element.50), channel_id=1, source_target_pairs={{16,0},{20,4},{24,8},{28,12},{0,16},{4,20},{8,24},{12,28},{17,1},{... | collective-permute-start | bytes 589832 | tf_op jit(solution)/shard_map/ppermute | solution.py:166
  165.8 12.0 %collective-permute-start.24 = (bf16[128,768]{1,0:T(8,128)(2,1)S(1)}, bf16[128,768]{1,0:T(8,128)(2,1)S(1)}, u32[]{:S(2)}, u32[]{:S(2)}) collective-permute-start(bf16[128,768]{1,0:T(8,128)(2,1)S(1)} %get-tuple-element.49), channel_id=1, source_target_pairs={{20,0},{16,4},{28,8},{24,12},{4,16},{0,20},{12,24},{8,28},{21,1},{... | collective-permute-start | bytes 589832 | tf_op jit(solution)/shard_map/ppermute | solution.py:166
  173.5 8.3 %collective-permute-start.14 = (bf16[128,768]{1,0:T(8,128)(2,1)S(1)}, bf16[128,768]{1,0:T(8,128)(2,1)S(1)}, u32[]{:S(2)}, u32[]{:S(2)}) collective-permute-start(bf16[128,768]{1,0:T(8,128)(2,1)S(1)} %get-tuple-element.52), channel_id=1, source_target_pairs={{8,0},{12,4},{16,8},{20,12},{24,16},{28,20},{0,24},{4,28},{9,1},{1... | collective-permute-start | bytes 589832 | tf_op jit(solution)/shard_map/ppermute | solution.py:166
  173.7 12.4 %collective-permute-start.15 = (bf16[128,768]{1,0:T(8,128)(2,1)S(1)}, bf16[128,768]{1,0:T(8,128)(2,1)S(1)}, u32[]{:S(2)}, u32[]{:S(2)}) collective-permute-start(bf16[128,768]{1,0:T(8,128)(2,1)S(1)} %get-tuple-element.51), channel_id=1, source_target_pairs={{12,0},{8,4},{20,8},{16,12},{28,16},{24,20},{4,24},{0,28},{13,1},{... | collective-permute-start | bytes 589832 | tf_op jit(solution)/shard_map/ppermute | solution.py:166
  174.7 11.4 %collective-permute-start.6 = (bf16[128,768]{1,0:T(8,128)(2,1)S(1)}, bf16[128,768]{1,0:T(8,128)(2,1)S(1)}, u32[]{:S(2)}, u32[]{:S(2)}) collective-permute-start(bf16[128,768]{1,0:T(8,128)(2,1)S(1)} %get-tuple-element.53), channel_id=1, source_target_pairs={{4,0},{0,4},{12,8},{8,12},{20,16},{16,20},{28,24},{24,28},{5,1},{1... | collective-permute-start | bytes 589832 | tf_op jit(solution)/shard_map/ppermute | solution.py:166

commit v2 on v1

v2 whole, which is shorter than its diff:
```python
import functools

import jax
import jax.numpy as jnp
from jax import lax
from jax.experimental import pallas as pl
from jax.experimental.pallas import tpu as pltpu
from jax.sharding import PartitionSpec as P

BF16 = jnp.bfloat16
F32 = jnp.float32
FREE = pl.CostEstimate(flops=0, bytes_accessed=0, transcendentals=0)


def pick_kernel(places, me, slot, routes_ref, tokens_ref, target_ref, *row_refs):
    count = routes_ref.shape[0]
    first, second = routes_ref[:, 0:1], routes_ref[:, 1:2]
    expert = lax.broadcasted_iota(jnp.int32, (count, 128), 1)
    is_first, is_second = expert == first, expert == second
    member = (is_first | is_second).astype(F32).astype(BF16)
    earlier = (
        lax.broadcasted_iota(jnp.int32, (count, count), 1) < lax.broadcasted_iota(jnp.int32, (count, count), 0)
    ).astype(F32).astype(BF16)
    before = jnp.dot(earlier, member, preferred_element_type=F32).astype(jnp.int32)
    index = me[0]
    high = (expert >> 1) - (index >> 1)
    place = jnp.where(high < 0, high + places // 2, high) * 2 + ((expert + index) & 1)
    spot = place * slot + before
    target_first = jnp.sum(jnp.where(is_first, spot, 0), axis=1, keepdims=True)
    target_second = jnp.sum(jnp.where(is_second, spot, 0), axis=1, keepdims=True)
    target_ref[:, 0:1] = target_first
    target_ref[:, 1:2] = target_second
    tokens = tokens_ref[...]
    for r in range(places):
        lane = lax.broadcasted_iota(jnp.int32, (count, slot), 1) + r * slot
        chosen = ((lane == target_first) | (lane == target_second)).astype(F32).astype(BF16)
        rows = lax.dot_general(chosen, tokens, (((0,), (0,)), ((), ())), preferred_element_type=F32)
        row_refs[r][...] = rows.astype(BF16)


def pick_rows(routes, tokens, me, slot, places):
    count, width = tokens.shape
    vmem = pl.BlockSpec(memory_space=pltpu.VMEM)

    def body(me_ref, *refs):
        pick_kernel(places, me_ref, slot, *refs)

    return pl.pallas_call(
        body,
        in_specs=[pl.BlockSpec(memory_space=pltpu.SMEM), vmem, vmem],
        out_specs=[vmem] * (places + 1),
        out_shape=[jax.ShapeDtypeStruct((count, 2), jnp.int32)]
        + [jax.ShapeDtypeStruct((slot, width), BF16)] * places,
        compiler_params=pltpu.CompilerParams(vmem_limit_bytes=24 << 20),
        cost_estimate=FREE,
        name="pick_rows",
    )(me, routes, tokens)


def combine_rows(target, gates, returned, slot):
    count = target.shape[0]
    width = returned[0].shape[1]
    vmem = pl.BlockSpec(memory_space=pltpu.VMEM)

    def body(target_ref, gates_ref, *refs):
        out_ref = refs[-1]
        total = None
        for k in range(2):
            picked = None
            for r, rows_ref in enumerate(refs[:-1]):
                lane = lax.broadcasted_iota(jnp.int32, (count, slot), 1) + r * slot
                chosen = (lane == target_ref[:, k : k + 1]).astype(F32).astype(BF16)
                part = jnp.dot(chosen, rows_ref[...], preferred_element_type=F32)
                picked = part if picked is None else picked + part
            weighted = gates_ref[:, k : k + 1] * picked
            total = weighted if total is None else total + weighted
        out_ref[...] = total.astype(BF16)

    return pl.pallas_call(
        body,
        in_specs=[vmem] * (2 + len(returned)),
        out_specs=vmem,
        out_shape=jax.ShapeDtypeStruct((count, width), BF16),
        compiler_params=pltpu.CompilerParams(vmem_limit_bytes=24 << 20),
        cost_estimate=FREE,
        name="combine_rows",
    )(target, gates, *returned)


def load(weights, after):
    n = len(weights)

    def body(*refs):
        copies = [pltpu.make_async_copy(refs[i], refs[n + 1 + i], refs[-1].at[i]) for i in range(n)]
        for copy in copies:
            copy.start()
        for copy in copies:
            copy.wait()

    return pl.pallas_call(
        body,
        in_specs=[pl.BlockSpec(memory_space=pltpu.HBM)] * n + [pl.BlockSpec(memory_space=pl.ANY)],
        out_specs=[pl.BlockSpec(memory_space=pltpu.VMEM)] * n,
        out_shape=[pltpu.VMEM(one.shape, one.dtype) for one in weights],
        scratch_shapes=[pltpu.SemaphoreType.DMA((n,))],
        compiler_params=pltpu.CompilerParams(vmem_limit_bytes=24 << 20),
        cost_estimate=FREE,
        name="load_weights",
    )(*[pltpu.with_memory_space_constraint(one, pltpu.HBM) for one in weights], after)


def feed_forward(order, pieces, up, down, after):
    n, waits = len(pieces), len(after)
    blocks = [len(piece) for piece in pieces]
    flat = [block for piece in pieces for block in piece]
    rows, width = sum(block.shape[0] for block in pieces[0]), flat[0].shape[1]
    hidden, features = down.shape
    half = n // 2

    def body(order_ref, *refs):
        piece_refs, up_ref, down_ref = list(refs[: len(flat)]), refs[len(flat)], refs[len(flat) + 1]
        near_refs, (far_ref, arrived, active) = refs[len(flat) + 2 + waits : -3], refs[-3:]
        starts = [pl.multiple_of(order_ref[i] * width, 128) for i in range(n)]
        for i in range(n):
            at = 0
            for _ in range(blocks[i]):
                block = piece_refs.pop(0)
                arrived[at : at + block.shape[0], pl.ds(starts[i], width)] = block[...]
                at += block.shape[0]
        raised = jnp.dot(arrived[...], up_ref[...], preferred_element_type=F32)
        active[...] = (0.5 * raised * (1.0 + jnp.tanh(0.5 * raised))).astype(BF16)
        for i in reversed(range(n)):
            value = jnp.dot(active[...], down_ref[:, pl.ds(starts[i], width)], preferred_element_type=F32)
            if i < half:
                near_refs[i][...] = value.astype(BF16)
            else:
                far_ref[i - half] = value.astype(BF16)

    vmem = pl.BlockSpec(memory_space=pltpu.VMEM)
    return pl.pallas_call(
        body,
        in_specs=[pl.BlockSpec(memory_space=pltpu.SMEM)]
        + [vmem] * (len(flat) + 2)
        + [pl.BlockSpec(memory_space=pl.ANY)] * waits,
        out_specs=[vmem] * (half + 1),
        scratch_shapes=[pltpu.VMEM((rows, features), BF16), pltpu.VMEM((rows, hidden), BF16)],
        out_shape=[jax.ShapeDtypeStruct((rows, width), BF16)] * half
        + [jax.ShapeDtypeStruct((half, rows, width), BF16)],
        compiler_params=pltpu.CompilerParams(vmem_limit_bytes=16 << 20),
        cost_estimate=FREE,
        name="feed_forward",
    )(order, *flat, *[pltpu.with_memory_space_constraint(one, pltpu.VMEM) for one in (up, down)], *after)


class Lane:
    def __init__(self, depth):
        self.depth, self.ended = depth, []

    def send(self, hop, *values):
        if len(self.ended) >= self.depth:
            values = lax.optimization_barrier((*values, *self.ended[-self.depth]))[: len(values)]
        self.ended.append([hop(value) if callable(hop) else hop[i](value) for i, value in enumerate(values)])
        return self.ended[-1]


def per_device(tokens, routes, route_gates, up_weight, down_weight):
    places, ranks = lax.axis_size("ep"), lax.axis_size("tp")
    count = tokens.shape[0]
    slot = 4 * count // places
    layers, planes = places // 2, ranks // 2
    group = max(1, min(layers, 256 // (2 * slot)))
    chunks = layers // group
    members = [range(chunk * 2 * group, (chunk + 1) * 2 * group) for chunk in range(chunks)]
    me, rank = lax.axis_index("ep"), lax.axis_index("tp")

    def ep_hop(place, back=False):
        far, flip = place // 2, place % 2
        pairs = [(i, (i // 2 + far) % layers * 2 + (i % 2 ^ flip)) for i in range(places)]
        return lambda value: lax.ppermute(value, "ep", [(b, a) for a, b in pairs] if back else pairs)

    def plane_hop(far):
        pairs = [(i, (i // 2 + far) % planes * 2 + i % 2) for i in range(ranks)]
        return lambda value: lax.ppermute(value, "tp", pairs)

    def core_hop(value):
        return lax.ppermute(value, "tp", [(i, i ^ 1) for i in range(ranks)])

    def gather(value):
        return plane_lane.send([plane_hop(far) for far in range(1, planes)], *[value] * (planes - 1))

    def join(values):
        return values[0] if len(values) == 1 else jnp.concatenate(values, axis=0)

    plane_lane, out_lane, back_lane = Lane(2), Lane(1), Lane(2)
    order = jnp.stack(
        [(rank // 2 - far) % planes * 2 + rank % 2 for far in range(planes)]
        + [(rank // 2 - far) % planes * 2 + (1 - rank % 2) for far in range(planes)]
    ).astype(jnp.int32)
    target, *picked = pick_rows(routes, tokens, me.reshape(1).astype(jnp.int32), slot, places)
    pieces, returned = [None] * chunks, [None] * places

    def fetch(chunk):
        places_of = [place for place in members[chunk] if place > 0]
        rows = [picked[place] for place in places_of]
        return out_lane.send([ep_hop(place) for place in places_of], *rows)

    def spread(chunk, own, across):
        same_core = [own, *across]
        pieces[chunk] = [[piece] for piece in same_core + [core_hop(piece) for piece in same_core]]

    def work(chunk):
        *near, stacked = feed_forward(order, pieces[chunk], up, down, [])
        crossed = core_hop(stacked)
        outgoing = [(near[far].astype(F32) + crossed[far].astype(F32)).astype(BF16) for far in range(1, planes)]
        summed = near[0].astype(F32) + crossed[0].astype(F32)
        for part in plane_lane.send([plane_hop(planes - far) for far in range(1, planes)], *outgoing):
            summed = summed + part.astype(F32)
        results = [summed[i * slot : (i + 1) * slot].astype(BF16) for i in range(len(members[chunk]))]
        if chunk == 0:
            returned[0] = results.pop(0)
        away = [place for place in members[chunk] if place > 0]
        for place, result in zip(away, back_lane.send([ep_hop(place, back=True) for place in away], *results)):
            returned[place] = result

    home = gather(picked[0])
    first, out_lane = fetch(0), Lane(1)
    across = gather(join(first))
    own = jnp.concatenate([picked[0], *first], axis=0)
    spread(0, own, [jnp.concatenate(pair, axis=0) for pair in zip(home, across)])
    for chunk in range(chunks):
        if chunk + 1 < chunks:
            own = join(fetch(chunk + 1))
            if chunk == 0:
                up, down = load([up_weight[0], down_weight[0]], own)
                spread(1, own, gather(own))
                work(0)
            else:
                spread(chunk + 1, own, gather(own))
                work(chunk)
        else:
            work(chunk)
    return combine_rows(target, route_gates, returned, slot)


def solution(mesh):
    in_specs = (
        P("ep", "tp"),
        P("ep", None),
        P("ep", None),
        P("ep", None, "tp"),
        P("ep", "tp", None),
    )
    out_specs = P("ep", "tp")
    return jax.shard_map(
        per_device, mesh=mesh, in_specs=in_specs, out_specs=out_specs, check_vma=False
    )
```

time: 189 us -> 140 us (0.74)
  Pallas kernels: 84.4 us -> 42.2 us
  starting transfers between devices: 37.2 us -> 31.2 us
  waiting for transfers between devices: 63.5 us -> 61.4 us
    pallas_call x4 -> x5, Pallas kernels: 80.7 us -> 38.4 us  [the longest x4 30.3 us: feed_forward(): pl.pallas_call(body, in_specs=[pl.BlockSpec(memory_space=pltpu.SMEM)] + [...]
    ppermute x8 -> x9, waiting for transfers between devices: 31.1 us -> 22.1 us  [plane_hop(): return lambda value: lax.ppermute(value, 'tp', pairs)]
    ppermute x14, waiting for transfers between devices: 32.4 us -> 39.3 us  [ep_hop(): lax.ppermute(value, 'ep', [(b, a) for a, b in pairs] if back else pairs)]
    ppermute x8 -> x9, starting transfers between devices: 13.5 us -> 10.2 us  [plane_hop(): return lambda value: lax.ppermute(value, 'tp', pairs)]
    ppermute x14, starting transfers between devices: 21 us -> 18.5 us  [ep_hop(): lax.ppermute(value, 'ep', [(b, a) for a, b in pairs] if back else pairs)]
  transfers between devices with their start and end apart: 34 -> 35, of which waited for: 11 -> 12; matrix products, arithmetic and copies ran while one was open for 1% -> 2% of each run, Pallas kernels for 43% -> 28%
where the time goes in v2:
time: 140 us; the launch traced here: 139 us
  waiting for transfers between devices  61.4 us (44%)
  Pallas kernels  42.2 us (30%)
  starting transfers between devices  31.2 us (22%)
  local copies, waits for them, and re-layouts  3.12 us (2%)
    ppermute x14, waiting for transfers between devices, ep_hop(): lax.ppermute(value, 'ep', [(b, a) for a, b in pairs] if back else pairs)  39.3 us
    pallas_call x4, Pallas kernels, feed_forward(): pl.pallas_call(body, in_specs=[pl.BlockSpec(memory_space=pltpu.SMEM)] + [...  30.3 us
    ppermute x9, waiting for transfers between devices, plane_hop(): return lambda value: lax.ppermute(value, 'tp', pairs)  22.1 us
    ppermute x14, starting transfers between devices, ep_hop(): lax.ppermute(value, 'ep', [(b, a) for a, b in pairs] if back else pairs)  18.5 us
    ppermute x9, starting transfers between devices, plane_hop(): return lambda value: lax.ppermute(value, 'tp', pairs)  10.2 us
    pallas_call x1, Pallas kernels, load(): pl.pallas_call(body, in_specs=[pl.BlockSpec(memory_space=pltpu.HBM)] * n...  8.17 us
  transfers between devices with their start and end apart: 35, of which 12 were waited for; matrix products, arithmetic and copies ran while one was open for 2% of the time, Pallas kernels for 28%

profile of v2, /device:TPU:0, one launch (start us, length us, event | category | flops | bytes accessed | tf_op | source)
XLA Modules:
  0.0 139.4 jit_solution(15949060479787445688)
XLA Ops:
  0.0 0.8 copy.6.refs_0_
  0.8 1.0 copy-done
  1.8 1.1 pick_rows.1
  3.0 3.0 %collective-permute-start = (bf16[128,768]{1,0:T(8,128)(2,1)S(1)}, bf16[128,768]{1,0:T(8,128)(2,1)S(1)}, u32[]{:S(2)}, u32[]{:S(2)}) collective-permute-start(bf16[128,768]{1,0:T(8,128)(2,1)S(1)} %get-tuple-element.45), channel_id=1, source_target_pairs={{0,4},{4,0},{8,12},{12,8},{16,20},{20,16},{24,28},{28,24},{1,5},{5... | collective-permute-start | bytes 589832 | tf_op jit(solution)/shard_map/ppermute | solution.py:179
  6.0 1.5 %collective-permute-start.1 = (bf16[128,768]{1,0:T(8,128)(2,1)S(1)}, bf16[128,768]{1,0:T(8,128)(2,1)S(1)}, u32[]{:S(2)}, u32[]{:S(2)}) collective-permute-start(bf16[128,768]{1,0:T(8,128)(2,1)S(1)} %get-tuple-element.44), channel_id=1, source_target_pairs={{0,2},{1,3},{2,0},{3,1},{4,6},{5,7},{6,4},{7,5},{8,10},{9,11},{10,... | collective-permute-start | bytes 589832 | tf_op jit(solution)/shard_map/ppermute | solution.py:183
  7.5 1.6 %collective-permute-start.5 = (bf16[128,768]{1,0:T(8,128)(2,1)S(1)}, bf16[128,768]{1,0:T(8,128)(2,1)S(1)}, u32[]{:S(2)}, u32[]{:S(2)}) collective-permute-start(bf16[128,768]{1,0:T(8,128)(2,1)S(1)} %get-tuple-element.46), channel_id=1, source_target_pairs={{0,8},{4,12},{8,16},{12,20},{16,24},{20,28},{24,0},{28,4},{1,9},{5... | collective-permute-start | bytes 589832 | tf_op jit(solution)/shard_map/ppermute | solution.py:179
  9.1 1.5 %collective-permute-start.6 = (bf16[128,768]{1,0:T(8,128)(2,1)S(1)}, bf16[128,768]{1,0:T(8,128)(2,1)S(1)}, u32[]{:S(2)}, u32[]{:S(2)}) collective-permute-start(bf16[128,768]{1,0:T(8,128)(2,1)S(1)} %get-tuple-element.47), channel_id=1, source_target_pairs={{0,12},{4,8},{8,20},{12,16},{16,28},{20,24},{24,4},{28,0},{1,13},{... | collective-permute-start | bytes 589832 | tf_op jit(solution)/shard_map/ppermute | solution.py:179
  10.6 0.2 collective-permute-done
  11.0 1.8 %collective-permute-start.2 = (bf16[128,768]{1,0:T(8,128)(2,1)S(1)}, bf16[128,768]{1,0:T(8,128)(2,1)S(1)}, u32[]{:S(2)}, u32[]{:S(2)}) collective-permute-start(bf16[128,768]{1,0:T(8,128)(2,1)S(1)} %collective-permute-done), channel_id=1, source_target_pairs={{0,2},{1,3},{2,0},{3,1},{4,6},{5,7},{6,4},{7,5},{8,10},{9,11},{10,... | collective-permute-start | bytes 589832 | tf_op jit(solution)/shard_map/ppermute | solution.py:183
  12.8 4.3 %collective-permute-done.5 = bf16[128,768]{1,0:T(8,128)(2,1)S(1)} collective-permute-done((bf16[128,768]{1,0:T(8,128)(2,1)S(1)}, bf16[128,768]{1,0:T(8,128)(2,1)S(1)}, u32[]{:S(2)}, u32[]{:S(2)}) %collective-permute-start.5) | collective-permute-done | bytes 196640 | tf_op jit(solution)/shard_map/ppermute | solution.py:179
  17.2 2.5 %collective-permute-done.6 = bf16[128,768]{1,0:T(8,128)(2,1)S(1)} collective-permute-done((bf16[128,768]{1,0:T(8,128)(2,1)S(1)}, bf16[128,768]{1,0:T(8,128)(2,1)S(1)}, u32[]{:S(2)}, u32[]{:S(2)}) %collective-permute-start.6) | collective-permute-done | bytes 196640 | tf_op jit(solution)/shard_map/ppermute | solution.py:179
  19.6 0.6 collective-permute-start.10
  20.2 0.7 collective-permute-start.17
  21.0 3.1 %collective-permute-start.18 = (bf16[128,768]{1,0:T(8,128)(2,1)S(1)}, bf16[128,768]{1,0:T(8,128)(2,1)}, u32[]{:S(2)}, u32[]{:S(2)}) collective-permute-start(bf16[128,768]{1,0:T(8,128)(2,1)S(1)} %get-tuple-element.62), channel_id=1, source_target_pairs={{0,20},{4,16},{8,28},{12,24},{16,4},{20,0},{24,12},{28,8},{1,21},{... | collective-permute-start | bytes 589832 | tf_op jit(solution)/shard_map/ppermute | solution.py:179
  24.3 8.2 %load_weights.1 = (bf16[3072,2048]{1,0:T(8,128)(2,1)S(1)}, bf16[2048,3072]{1,0:T(8,128)(2,1)S(1)}) custom-call(bf16[3072,2048]{1,0:T(8,128)(2,1)} %bitcast.47, bf16[2048,3072]{1,0:T(8,128)(2,1)} %bitcast.48, bf16[256,768]{1,0:T(8,128)(2,1)S(1)} %constant_dynamic-update-slice_fusion.4.refs_2_.refs_0_), custom_call_target="tpu_custom_call" | custom-call | tf_op jit(solution)/shard_map/load_weights/pallas_call | solution.py:100
  32.5 2.0 %collective-permute-done.17 = bf16[128,768]{1,0:T(8,128)(2,1)S(1)} collective-permute-done((bf16[128,768]{1,0:T(8,128)(2,1)S(1)}, bf16[128,768]{1,0:T(8,128)(2,1)S(1)}, u32[]{:S(2)}, u32[]{:S(2)}) %collective-permute-start.17) | collective-permute-done | bytes 196640 | tf_op jit(solution)/shard_map/ppermute | solution.py:179
  34.5 4.3 %collective-permute-done.18 = bf16[128,768]{1,0:T(8,128)(2,1)} collective-permute-done((bf16[128,768]{1,0:T(8,128)(2,1)S(1)}, bf16[128,768]{1,0:T(8,128)(2,1)}, u32[]{:S(2)}, u32[]{:S(2)}) %collective-permute-start.18) | collective-permute-done | bytes 196640 | tf_op jit(solution)/shard_map/ppermute | solution.py:179
  38.8 2.5 %collective-permute-start.26 = (bf16[128,768]{1,0:T(8,128)(2,1)S(1)}, bf16[128,768]{1,0:T(8,128)(2,1)S(1)}, u32[]{:S(2)}, u32[]{:S(2)}) collective-permute-start(bf16[128,768]{1,0:T(8,128)(2,1)S(1)} %get-tuple-element.72), channel_id=1, source_target_pairs={{0,24},{4,28},{8,0},{12,4},{16,8},{20,12},{24,16},{28,20},{1,25},{... | collective-permute-start | bytes 589832 | tf_op jit(solution)/shard_map/ppermute | solution.py:179
  41.3 0.9 constant_dynamic-update-slice_fusion.6.refs_0_
  42.3 1.6 %collective-permute-start.19 = (bf16[256,768]{1,0:T(8,128)(2,1)S(1)}, bf16[256,768]{1,0:T(8,128)(2,1)S(1)}, u32[]{:S(2)}, u32[]{:S(2)}) collective-permute-start(bf16[256,768]{1,0:T(8,128)(2,1)S(1)} %constant_dynamic-update-slice_fusion.6.refs_0_), channel_id=1, source_target_pairs={{0,2},{1,3},{2,0},{3,1},{4,6},{5,7},{6,4},{7,5},{8,10},{9,11},{10,... | collective-permute-start | bytes 1179656 | tf_op jit(solution)/shard_map/ppermute | solution.py:183
  43.9 7.5 %feed_forward.4 = (bf16[256,768]{1,0:T(8,128)(2,1)S(1)}, bf16[256,768]{1,0:T(8,128)(2,1)S(1)}, bf16[2,256,768]{2,1,0:T(8,128)(2,1)S(1)}) custom-call(s32[4]{0:T(128)S(1)} %pad_add_fusion.order_ref, bf16[256,768]{1,0:T(8,128)(2,1)S(1)} %constant_dynamic-update-slice_fusion.refs_0_, bf16[256,768]{1,0:T(8,128)(2,1)S(1)} %constant_dynamic-update-slice_fusion.2.refs_1_, ...), custom_call_target="tpu_custom_call" | custom-call | tf_op jit(solution)/shard_map/feed_forward/pallas_call | solution.py:140
  51.5 0.5 collective-permute-start.11
  52.1 8.1 %collective-permute-done.27 = bf16[128,768]{1,0:T(8,128)(2,1)S(1)} collective-permute-done((bf16[128,768]{1,0:T(8,128)(2,1)S(1)}, bf16[128,768]{1,0:T(8,128)(2,1)S(1)}, u32[]{:S(2)}, u32[]{:S(2)}) %collective-permute-start.27) | collective-permute-done | bytes 196640 | tf_op jit(solution)/shard_map/ppermute | solution.py:179
  60.2 0.6 collective-permute-start.28
  60.8 7.5 %feed_forward.5 = (bf16[256,768]{1,0:T(8,128)(2,1)S(1)}, bf16[256,768]{1,0:T(8,128)(2,1)S(1)}, bf16[2,256,768]{2,1,0:T(8,128)(2,1)S(1)}) custom-call(s32[4]{0:T(128)S(1)} %pad_add_fusion.order_ref, bf16[256,768]{1,0:T(8,128)(2,1)S(1)} %constant_dynamic-update-slice_fusion.4.refs_2_.refs_0_, bf16[256,768]{1,0:T(8,128)(2,1)S(1)} %collective-permute-done.10.refs_1_, ...), custom_call_target="tpu_custom_call" | custom-call | tf_op jit(solution)/shard_map/feed_forward/pallas_call | solution.py:140
  68.4 0.5 collective-permute-start.20
  69.0 2.0 %collective-permute-done.28.refs_1_ = bf16[256,768]{1,0:T(8,128)(2,1)S(1)} collective-permute-done((bf16[256,768]{1,0:T(8,128)(2,1)S(1)}, bf16[256,768]{1,0:T(8,128)(2,1)S(1)}, u32[]{:S(2)}, u32[]{:S(2)}) %collective-permute-start.28) | collective-permute-done | bytes 393248 | tf_op jit(solution)/shard_map/ppermute | solution.py:183
  71.0 0.5 collective-permute-start.30
  71.6 1.2 collective-permute-start.8
  72.7 7.5 %feed_forward.6 = (bf16[256,768]{1,0:T(8,128)(2,1)S(1)}, bf16[256,768]{1,0:T(8,128)(2,1)S(1)}, bf16[2,256,768]{2,1,0:T(8,128)(2,1)S(1)}) custom-call(s32[4]{0:T(128)S(1)} %pad_add_fusion.order_ref, bf16[256,768]{1,0:T(8,128)(2,1)S(1)} %constant_dynamic-update-slice_fusion.6.refs_0_, bf16[256,768]{1,0:T(8,128)(2,1)S(1)} %collective-permute-done.19.refs_1_, ...), custom_call_target="tpu_custom_call" | custom-call | tf_op jit(solution)/shard_map/feed_forward/pallas_call | solution.py:140
  80.4 7.7 %feed_forward.7 = (bf16[256,768]{1,0:T(8,128)(2,1)S(1)}, bf16[256,768]{1,0:T(8,128)(2,1)S(1)}, bf16[2,256,768]{2,1,0:T(8,128)(2,1)S(1)}) custom-call(s32[4]{0:T(128)S(1)} %pad_add_fusion.order_ref, bf16[256,768]{1,0:T(8,128)(2,1)S(1)} %constant_dynamic-update-slice_fusion.8.refs_0_, bf16[256,768]{1,0:T(8,128)(2,1)S(1)} %collective-permute-done.28.refs_1_, ...), custom_call_target="tpu_custom_call" | custom-call | tf_op jit(solution)/shard_map/feed_forward/pallas_call | solution.py:140
  88.1 0.6 collective-permute-start.31
  88.8 1.0 collective-permute-start.14
  89.8 0.2 fusion.11
  90.0 0.6 collective-permute-start.9
  90.7 9.2 %collective-permute-done.14 = bf16[256,768]{1,0:T(8,128)(2,1)S(1)} collective-permute-done((bf16[256,768]{1,0:T(8,128)(2,1)S(1)}, bf16[256,768]{1,0:T(8,128)(2,1)S(1)}, u32[]{:S(2)}, u32[]{:S(2)}) %collective-permute-start.14) | collective-permute-done | bytes 393248 | tf_op jit(solution)/shard_map/ppermute | solution.py:183
  99.9 0.9 collective-permute-start.23
  100.8 0.2 fusion.8
  101.0 1.9 %collective-permute-start.15 = (bf16[128,768]{1,0:T(8,128)(2,1)S(1)}, bf16[128,768]{1,0:T(8,128)(2,1)S(1)}, u32[]{:S(2)}, u32[]{:S(2)}) collective-permute-start(bf16[128,768]{1,0:T(8,128)(2,1)S(1)} %get-tuple-element.86), channel_id=1, source_target_pairs={{8,0},{12,4},{16,8},{20,12},{24,16},{28,20},{0,24},{4,28},{9,1},{1... | collective-permute-start | bytes 589832 | tf_op jit(solution)/shard_map/ppermute | solution.py:179
  102.9 0.5 collective-permute-start.16
  103.5 1.0 collective-permute-start.32
  104.5 7.5 %collective-permute-done.23 = bf16[256,768]{1,0:T(8,128)(2,1)S(1)} collective-permute-done((bf16[256,768]{1,0:T(8,128)(2,1)S(1)}, bf16[256,768]{1,0:T(8,128)(2,1)S(1)}, u32[]{:S(2)}, u32[]{:S(2)}) %collective-permute-start.23) | collective-permute-done | bytes 393248 | tf_op jit(solution)/shard_map/ppermute | solution.py:183
  111.9 0.2 fusion.5
  112.2 2.9 %collective-permute-start.25 = (bf16[128,768]{1,0:T(8,128)(2,1)S(1)}, bf16[128,768]{1,0:T(8,128)(2,1)S(1)}, u32[]{:S(2)}, u32[]{:S(2)}) collective-permute-start(bf16[128,768]{1,0:T(8,128)(2,1)S(1)} %get-tuple-element.69), channel_id=1, source_target_pairs={{20,0},{16,4},{28,8},{24,12},{4,16},{0,20},{12,24},{8,28},{21,1},{... | collective-permute-start | bytes 589832 | tf_op jit(solution)/shard_map/ppermute | solution.py:179
  115.1 3.4 %collective-permute-done.32 = bf16[256,768]{1,0:T(8,128)(2,1)S(1)} collective-permute-done((bf16[256,768]{1,0:T(8,128)(2,1)S(1)}, bf16[256,768]{1,0:T(8,128)(2,1)S(1)}, u32[]{:S(2)}, u32[]{:S(2)}) %collective-permute-start.32) | collective-permute-done | bytes 393248 | tf_op jit(solution)/shard_map/ppermute | solution.py:183
  119.0 14.0 %collective-permute-done.24.refs_4_ = bf16[128,768]{1,0:T(8,128)(2,1)S(1)} collective-permute-done((bf16[128,768]{1,0:T(8,128)(2,1)S(1)}, bf16[128,768]{1,0:T(8,128)(2,1)S(1)}, u32[]{:S(2)}, u32[]{:S(2)}) %collective-permute-start.24) | collective-permute-done | bytes 196640 | tf_op jit(solution)/shard_map/ppermute | solution.py:179
  133.0 3.8 %collective-permute-done.25.refs_5_ = bf16[128,768]{1,0:T(8,128)(2,1)S(1)} collective-permute-done((bf16[128,768]{1,0:T(8,128)(2,1)S(1)}, bf16[128,768]{1,0:T(8,128)(2,1)S(1)}, u32[]{:S(2)}, u32[]{:S(2)}) %collective-permute-start.25) | collective-permute-done | bytes 196640 | tf_op jit(solution)/shard_map/ppermute | solution.py:179
  136.8 2.6 %combine_rows.1 = bf16[256,768]{1,0:T(8,128)(2,1)} custom-call(s32[256,2]{1,0:T(8,128)S(1)} %get-tuple-element.43.target_ref, f32[256,2]{1,0:T(8,128)S(1)} %copy.7.gates_ref, bf16[128,768]{1,0:T(8,128)(2,1)S(1)} %get-tuple-element.88.refs_0_, bf16[128,768]{1,0:T(8,128)(2,1)S(1)} %collective-permute-done.9.refs_1_, ...), custom_call_target="tpu_custom_call" | custom-call | tf_op jit(solution)/shard_map/combine_rows/pallas_call | solution.py:79
  (58 shorter events, 1.8 us)
Async XLA Ops:
  0.8 1.0 copy-start
  3.0 7.9 %collective-permute-start = (bf16[128,768]{1,0:T(8,128)(2,1)S(1)}, bf16[128,768]{1,0:T(8,128)(2,1)S(1)}, u32[]{:S(2)}, u32[]{:S(2)}) collective-permute-start(bf16[128,768]{1,0:T(8,128)(2,1)S(1)} %get-tuple-element.45), channel_id=1, source_target_pairs={{0,4},{4,0},{8,12},{12,8},{16,20},{20,16},{24,28},{28,24},{1,5},{5... | collective-permute-start | bytes 589832 | tf_op jit(solution)/shard_map/ppermute | solution.py:179
  6.0 13.7 %collective-permute-start.1 = (bf16[128,768]{1,0:T(8,128)(2,1)S(1)}, bf16[128,768]{1,0:T(8,128)(2,1)S(1)}, u32[]{:S(2)}, u32[]{:S(2)}) collective-permute-start(bf16[128,768]{1,0:T(8,128)(2,1)S(1)} %get-tuple-element.44), channel_id=1, source_target_pairs={{0,2},{1,3},{2,0},{3,1},{4,6},{5,7},{6,4},{7,5},{8,10},{9,11},{10,... | collective-permute-start | bytes 589832 | tf_op jit(solution)/shard_map/ppermute | solution.py:183
  7.5 9.6 %collective-permute-start.5 = (bf16[128,768]{1,0:T(8,128)(2,1)S(1)}, bf16[128,768]{1,0:T(8,128)(2,1)S(1)}, u32[]{:S(2)}, u32[]{:S(2)}) collective-permute-start(bf16[128,768]{1,0:T(8,128)(2,1)S(1)} %get-tuple-element.46), channel_id=1, source_target_pairs={{0,8},{4,12},{8,16},{12,20},{16,24},{20,28},{24,0},{28,4},{1,9},{5... | collective-permute-start | bytes 589832 | tf_op jit(solution)/shard_map/ppermute | solution.py:179
  9.1 10.5 %collective-permute-start.6 = (bf16[128,768]{1,0:T(8,128)(2,1)S(1)}, bf16[128,768]{1,0:T(8,128)(2,1)S(1)}, u32[]{:S(2)}, u32[]{:S(2)}) collective-permute-start(bf16[128,768]{1,0:T(8,128)(2,1)S(1)} %get-tuple-element.47), channel_id=1, source_target_pairs={{0,12},{4,8},{8,20},{12,16},{16,28},{20,24},{24,4},{28,0},{1,13},{... | collective-permute-start | bytes 589832 | tf_op jit(solution)/shard_map/ppermute | solution.py:179
  10.9 33.0 %collective-permute-start.3 = (bf16[256,768]{1,0:T(8,128)(2,1)S(1)}, bf16[256,768]{1,0:T(8,128)(2,1)S(1)}, u32[]{:S(2)}, u32[]{:S(2)}) collective-permute-start(bf16[256,768]{1,0:T(8,128)(2,1)S(1)} %constant_dynamic-update-slice_fusion.refs_0_), channel_id=1, source_target_pairs={{0,1},{1,0},{2,3},{3,2},{4,5},{5,4},{6,7},{7,6},{8,9},{9,8},{10,11... | collective-permute-start | bytes 1179656 | tf_op jit(solution)/shard_map/ppermute | solution.py:186
  11.0 13.1 %collective-permute-start.2 = (bf16[128,768]{1,0:T(8,128)(2,1)S(1)}, bf16[128,768]{1,0:T(8,128)(2,1)S(1)}, u32[]{:S(2)}, u32[]{:S(2)}) collective-permute-start(bf16[128,768]{1,0:T(8,128)(2,1)S(1)} %collective-permute-done), channel_id=1, source_target_pairs={{0,2},{1,3},{2,0},{3,1},{4,6},{5,7},{6,4},{7,5},{8,10},{9,11},{10,... | collective-permute-start | bytes 589832 | tf_op jit(solution)/shard_map/ppermute | solution.py:183
  19.6 22.6 %collective-permute-start.10 = (bf16[256,768]{1,0:T(8,128)(2,1)S(1)}, bf16[256,768]{1,0:T(8,128)(2,1)S(1)}, u32[]{:S(2)}, u32[]{:S(2)}) collective-permute-start(bf16[256,768]{1,0:T(8,128)(2,1)S(1)} %constant_dynamic-update-slice_fusion.4.refs_2_.refs_0_), channel_id=1, source_target_pairs={{0,2},{1,3},{2,0},{3,1},{4,6},{5,7},{6,4},{7,5},{8,10},{9,11},{10,... | collective-permute-start | bytes 1179656 | tf_op jit(solution)/shard_map/ppermute | solution.py:183
  20.2 14.3 %collective-permute-start.17 = (bf16[128,768]{1,0:T(8,128)(2,1)S(1)}, bf16[128,768]{1,0:T(8,128)(2,1)S(1)}, u32[]{:S(2)}, u32[]{:S(2)}) collective-permute-start(bf16[128,768]{1,0:T(8,128)(2,1)S(1)} %get-tuple-element.61), channel_id=1, source_target_pairs={{0,16},{4,20},{8,24},{12,28},{16,0},{20,4},{24,8},{28,12},{1,17},{... | collective-permute-start | bytes 589832 | tf_op jit(solution)/shard_map/ppermute | solution.py:179
  21.0 17.9 %collective-permute-start.18 = (bf16[128,768]{1,0:T(8,128)(2,1)S(1)}, bf16[128,768]{1,0:T(8,128)(2,1)}, u32[]{:S(2)}, u32[]{:S(2)}) collective-permute-start(bf16[128,768]{1,0:T(8,128)(2,1)S(1)} %get-tuple-element.62), channel_id=1, source_target_pairs={{0,20},{4,16},{8,28},{12,24},{16,4},{20,0},{24,12},{28,8},{1,21},{... | collective-permute-start | bytes 589832 | tf_op jit(solution)/shard_map/ppermute | solution.py:179
  24.1 19.7 %collective-permute-start.4 = (bf16[256,768]{1,0:T(8,128)(2,1)S(1)}, bf16[256,768]{1,0:T(8,128)(2,1)S(1)}, u32[]{:S(2)}, u32[]{:S(2)}) collective-permute-start(bf16[256,768]{1,0:T(8,128)(2,1)S(1)} %constant_dynamic-update-slice_fusion.2.refs_1_), channel_id=1, source_target_pairs={{0,1},{1,0},{2,3},{3,2},{4,5},{5,4},{6,7},{7,6},{8,9},{9,8},{10,11... | collective-permute-start | bytes 1179656 | tf_op jit(solution)/shard_map/ppermute | solution.py:186
  38.8 13.2 %collective-permute-start.26 = (bf16[128,768]{1,0:T(8,128)(2,1)S(1)}, bf16[128,768]{1,0:T(8,128)(2,1)S(1)}, u32[]{:S(2)}, u32[]{:S(2)}) collective-permute-start(bf16[128,768]{1,0:T(8,128)(2,1)S(1)} %get-tuple-element.72), channel_id=1, source_target_pairs={{0,24},{4,28},{8,0},{12,4},{16,8},{20,12},{24,16},{28,20},{1,25},{... | collective-permute-start | bytes 589832 | tf_op jit(solution)/shard_map/ppermute | solution.py:179
  42.3 17.9 %collective-permute-start.19 = (bf16[256,768]{1,0:T(8,128)(2,1)S(1)}, bf16[256,768]{1,0:T(8,128)(2,1)S(1)}, u32[]{:S(2)}, u32[]{:S(2)}) collective-permute-start(bf16[256,768]{1,0:T(8,128)(2,1)S(1)} %constant_dynamic-update-slice_fusion.6.refs_0_), channel_id=1, source_target_pairs={{0,2},{1,3},{2,0},{3,1},{4,6},{5,7},{6,4},{7,5},{8,10},{9,11},{10,... | collective-permute-start | bytes 1179656 | tf_op jit(solution)/shard_map/ppermute | solution.py:183
  51.4 19.6 %collective-permute-start.7 = (bf16[2,256,768]{2,1,0:T(8,128)(2,1)S(1)}, bf16[2,256,768]{2,1,0:T(8,128)(2,1)S(1)}, u32[]{:S(2)}, u32[]{:S(2)}) collective-permute-start(bf16[2,256,768]{2,1,0:T(8,128)(2,1)S(1)} %get-tuple-element.51), channel_id=1, source_target_pairs={{0,1},{1,0},{2,3},{3,2},{4,5},{5,4},{6,7},{7,6},{8,9},{9,8},{10,11... | collective-permute-start | bytes 2359304 | tf_op jit(solution)/shard_map/ppermute | solution.py:186
  51.5 9.3 %collective-permute-start.11 = (bf16[256,768]{1,0:T(8,128)(2,1)S(1)}, bf16[256,768]{1,0:T(8,128)(2,1)S(1)}, u32[]{:S(2)}, u32[]{:S(2)}) collective-permute-start(bf16[256,768]{1,0:T(8,128)(2,1)S(1)} %constant_dynamic-update-slice_fusion.4.refs_2_.refs_0_), channel_id=1, source_target_pairs={{0,1},{1,0},{2,3},{3,2},{4,5},{5,4},{6,7},{7,6},{8,9},{9,8},{10,11... | collective-permute-start | bytes 1179656 | tf_op jit(solution)/shard_map/ppermute | solution.py:186
  51.9 8.9 %collective-permute-start.12 = (bf16[256,768]{1,0:T(8,128)(2,1)S(1)}, bf16[256,768]{1,0:T(8,128)(2,1)S(1)}, u32[]{:S(2)}, u32[]{:S(2)}) collective-permute-start(bf16[256,768]{1,0:T(8,128)(2,1)S(1)} %collective-permute-done.10.refs_1_), channel_id=1, source_target_pairs={{0,1},{1,0},{2,3},{3,2},{4,5},{5,4},{6,7},{7,6},{8,9},{9,8},{10,11... | collective-permute-start | bytes 1179656 | tf_op jit(solution)/shard_map/ppermute | solution.py:186
  52.0 8.2 %collective-permute-start.27 = (bf16[128,768]{1,0:T(8,128)(2,1)S(1)}, bf16[128,768]{1,0:T(8,128)(2,1)S(1)}, u32[]{:S(2)}, u32[]{:S(2)}) collective-permute-start(bf16[128,768]{1,0:T(8,128)(2,1)S(1)} %get-tuple-element.73), channel_id=1, source_target_pairs={{0,28},{4,24},{8,4},{12,0},{16,12},{20,8},{24,20},{28,16},{1,29},{... | collective-permute-start | bytes 589832 | tf_op jit(solution)/shard_map/ppermute | solution.py:179
  60.2 10.7 %collective-permute-start.28 = (bf16[256,768]{1,0:T(8,128)(2,1)S(1)}, bf16[256,768]{1,0:T(8,128)(2,1)S(1)}, u32[]{:S(2)}, u32[]{:S(2)}) collective-permute-start(bf16[256,768]{1,0:T(8,128)(2,1)S(1)} %constant_dynamic-update-slice_fusion.8.refs_0_), channel_id=1, source_target_pairs={{0,2},{1,3},{2,0},{3,1},{4,6},{5,7},{6,4},{7,5},{8,10},{9,11},{10,... | collective-permute-start | bytes 1179656 | tf_op jit(solution)/shard_map/ppermute | solution.py:183
  68.3 20.4 %collective-permute-start.13 = (bf16[2,256,768]{2,1,0:T(8,128)(2,1)S(1)}, bf16[2,256,768]{2,1,0:T(8,128)(2,1)S(1)}, u32[]{:S(2)}, u32[]{:S(2)}) collective-permute-start(bf16[2,256,768]{2,1,0:T(8,128)(2,1)S(1)} %get-tuple-element.56), channel_id=1, source_target_pairs={{0,1},{1,0},{2,3},{3,2},{4,5},{5,4},{6,7},{7,6},{8,9},{9,8},{10,11... | collective-permute-start | bytes 2359304 | tf_op jit(solution)/shard_map/ppermute | solution.py:186
  68.4 3.2 %collective-permute-start.20 = (bf16[256,768]{1,0:T(8,128)(2,1)S(1)}, bf16[256,768]{1,0:T(8,128)(2,1)S(1)}, u32[]{:S(2)}, u32[]{:S(2)}) collective-permute-start(bf16[256,768]{1,0:T(8,128)(2,1)S(1)} %constant_dynamic-update-slice_fusion.6.refs_0_), channel_id=1, source_target_pairs={{0,1},{1,0},{2,3},{3,2},{4,5},{5,4},{6,7},{7,6},{8,9},{9,8},{10,11... | collective-permute-start | bytes 1179656 | tf_op jit(solution)/shard_map/ppermute | solution.py:186
  68.9 3.9 %collective-permute-start.21 = (bf16[256,768]{1,0:T(8,128)(2,1)S(1)}, bf16[256,768]{1,0:T(8,128)(2,1)S(1)}, u32[]{:S(2)}, u32[]{:S(2)}) collective-permute-start(bf16[256,768]{1,0:T(8,128)(2,1)S(1)} %collective-permute-done.19.refs_1_), channel_id=1, source_target_pairs={{0,1},{1,0},{2,3},{3,2},{4,5},{5,4},{6,7},{7,6},{8,9},{9,8},{10,11... | collective-permute-start | bytes 1179656 | tf_op jit(solution)/shard_map/ppermute | solution.py:186
  71.0 9.4 %collective-permute-start.29 = (bf16[256,768]{1,0:T(8,128)(2,1)S(1)}, bf16[256,768]{1,0:T(8,128)(2,1)S(1)}, u32[]{:S(2)}, u32[]{:S(2)}) collective-permute-start(bf16[256,768]{1,0:T(8,128)(2,1)S(1)} %constant_dynamic-update-slice_fusion.8.refs_0_), channel_id=1, source_target_pairs={{0,1},{1,0},{2,3},{3,2},{4,5},{5,4},{6,7},{7,6},{8,9},{9,8},{10,11... | collective-permute-start | bytes 1179656 | tf_op jit(solution)/shard_map/ppermute | solution.py:186
  71.0 9.4 %collective-permute-start.30 = (bf16[256,768]{1,0:T(8,128)(2,1)S(1)}, bf16[256,768]{1,0:T(8,128)(2,1)S(1)}, u32[]{:S(2)}, u32[]{:S(2)}) collective-permute-start(bf16[256,768]{1,0:T(8,128)(2,1)S(1)} %collective-permute-done.28.refs_1_), channel_id=1, source_target_pairs={{0,1},{1,0},{2,3},{3,2},{4,5},{5,4},{6,7},{7,6},{8,9},{9,8},{10,11... | collective-permute-start | bytes 1179656 | tf_op jit(solution)/shard_map/ppermute | solution.py:186
  71.6 17.2 %collective-permute-start.8 = (bf16[256,768]{1,0:T(8,128)(2,1)S(1)}, bf16[256,768]{1,0:T(8,128)(2,1)S(1)}, u32[]{:S(2)}, u32[]{:S(2)}) collective-permute-start(bf16[256,768]{1,0:T(8,128)(2,1)S(1)} %fusion.9), channel_id=1, source_target_pairs={{0,2},{1,3},{2,0},{3,1},{4,6},{5,7},{6,4},{7,5},{8,10},{9,11},{10,... | collective-permute-start | bytes 1179656 | tf_op jit(solution)/shard_map/ppermute | solution.py:183
  80.3 10.3 %collective-permute-start.22 = (bf16[2,256,768]{2,1,0:T(8,128)(2,1)S(1)}, bf16[2,256,768]{2,1,0:T(8,128)(2,1)S(1)}, u32[]{:S(2)}, u32[]{:S(2)}) collective-permute-start(bf16[2,256,768]{2,1,0:T(8,128)(2,1)S(1)} %get-tuple-element.65), channel_id=1, source_target_pairs={{0,1},{1,0},{2,3},{3,2},{4,5},{5,4},{6,7},{7,6},{8,9},{9,8},{10,11... | collective-permute-start | bytes 2359304 | tf_op jit(solution)/shard_map/ppermute | solution.py:186
  88.1 30.8 %copy-start.1 = (f32[256,2]{0,1:T(2,128)S(1)}, f32[256,2]{0,1:T(2,128)}, u32[]{:S(2)}) copy-start(f32[256,2]{0,1:T(2,128)} %param.7) | copy-start | bytes 6148
  88.1 15.3 %collective-permute-start.31 = (bf16[2,256,768]{2,1,0:T(8,128)(2,1)S(1)}, bf16[2,256,768]{2,1,0:T(8,128)(2,1)S(1)}, u32[]{:S(2)}, u32[]{:S(2)}) collective-permute-start(bf16[2,256,768]{2,1,0:T(8,128)(2,1)S(1)} %get-tuple-element.76), channel_id=1, source_target_pairs={{0,1},{1,0},{2,3},{3,2},{4,5},{5,4},{6,7},{7,6},{8,9},{9,8},{10,11... | collective-permute-start | bytes 2359304 | tf_op jit(solution)/shard_map/ppermute | solution.py:186
  88.8 11.1 %collective-permute-start.14 = (bf16[256,768]{1,0:T(8,128)(2,1)S(1)}, bf16[256,768]{1,0:T(8,128)(2,1)S(1)}, u32[]{:S(2)}, u32[]{:S(2)}) collective-permute-start(bf16[256,768]{1,0:T(8,128)(2,1)S(1)} %fusion.6), channel_id=1, source_target_pairs={{0,2},{1,3},{2,0},{3,1},{4,6},{5,7},{6,4},{7,5},{8,10},{9,11},{10,... | collective-permute-start | bytes 1179656 | tf_op jit(solution)/shard_map/ppermute | solution.py:183
  90.0 22.2 %collective-permute-start.9 = (bf16[128,768]{1,0:T(8,128)(2,1)S(1)}, bf16[128,768]{1,0:T(8,128)(2,1)S(1)}, u32[]{:S(2)}, u32[]{:S(2)}) collective-permute-start(bf16[128,768]{1,0:T(8,128)(2,1)S(1)} %get-tuple-element.87), channel_id=1, source_target_pairs={{4,0},{0,4},{12,8},{8,12},{20,16},{16,20},{28,24},{24,28},{5,1},{1... | collective-permute-start | bytes 589832 | tf_op jit(solution)/shard_map/ppermute | solution.py:179
  99.9 12.1 %collective-permute-start.23 = (bf16[256,768]{1,0:T(8,128)(2,1)S(1)}, bf16[256,768]{1,0:T(8,128)(2,1)S(1)}, u32[]{:S(2)}, u32[]{:S(2)}) collective-permute-start(bf16[256,768]{1,0:T(8,128)(2,1)S(1)} %fusion.3), channel_id=1, source_target_pairs={{0,2},{1,3},{2,0},{3,1},{4,6},{5,7},{6,4},{7,5},{8,10},{9,11},{10,... | collective-permute-start | bytes 1179656 | tf_op jit(solution)/shard_map/ppermute | solution.py:183
  101.0 17.7 %collective-permute-start.15 = (bf16[128,768]{1,0:T(8,128)(2,1)S(1)}, bf16[128,768]{1,0:T(8,128)(2,1)S(1)}, u32[]{:S(2)}, u32[]{:S(2)}) collective-permute-start(bf16[128,768]{1,0:T(8,128)(2,1)S(1)} %get-tuple-element.86), channel_id=1, source_target_pairs={{8,0},{12,4},{16,8},{20,12},{24,16},{28,20},{0,24},{4,28},{9,1},{1... | collective-permute-start | bytes 589832 | tf_op jit(solution)/shard_map/ppermute | solution.py:179
  102.9 15.8 %collective-permute-start.16 = (bf16[128,768]{1,0:T(8,128)(2,1)S(1)}, bf16[128,768]{1,0:T(8,128)(2,1)S(1)}, u32[]{:S(2)}, u32[]{:S(2)}) collective-permute-start(bf16[128,768]{1,0:T(8,128)(2,1)S(1)} %get-tuple-element.85), channel_id=1, source_target_pairs={{12,0},{8,4},{20,8},{16,12},{28,16},{24,20},{4,24},{0,28},{13,1},{... | collective-permute-start | bytes 589832 | tf_op jit(solution)/shard_map/ppermute | solution.py:179
  103.5 15.0 %collective-permute-start.32 = (bf16[256,768]{1,0:T(8,128)(2,1)S(1)}, bf16[256,768]{1,0:T(8,128)(2,1)S(1)}, u32[]{:S(2)}, u32[]{:S(2)}) collective-permute-start(bf16[256,768]{1,0:T(8,128)(2,1)S(1)} %fusion), channel_id=1, source_target_pairs={{0,2},{1,3},{2,0},{3,1},{4,6},{5,7},{6,4},{7,5},{8,10},{9,11},{10,... | collective-permute-start | bytes 1179656 | tf_op jit(solution)/shard_map/ppermute | solution.py:183
  112.1 20.9 %collective-permute-start.24 = (bf16[128,768]{1,0:T(8,128)(2,1)S(1)}, bf16[128,768]{1,0:T(8,128)(2,1)S(1)}, u32[]{:S(2)}, u32[]{:S(2)}) collective-permute-start(bf16[128,768]{1,0:T(8,128)(2,1)S(1)} %get-tuple-element.68), channel_id=1, source_target_pairs={{16,0},{20,4},{24,8},{28,12},{0,16},{4,20},{8,24},{12,28},{17,1},{... | collective-permute-start | bytes 589832 | tf_op jit(solution)/shard_map/ppermute | solution.py:179
  112.2 24.6 %collective-permute-start.25 = (bf16[128,768]{1,0:T(8,128)(2,1)S(1)}, bf16[128,768]{1,0:T(8,128)(2,1)S(1)}, u32[]{:S(2)}, u32[]{:S(2)}) collective-permute-start(bf16[128,768]{1,0:T(8,128)(2,1)S(1)} %get-tuple-element.69), channel_id=1, source_target_pairs={{20,0},{16,4},{28,8},{24,12},{4,16},{0,20},{12,24},{8,28},{21,1},{... | collective-permute-start | bytes 589832 | tf_op jit(solution)/shard_map/ppermute | solution.py:179
  118.7 18.1 %collective-permute-start.33 = (bf16[128,768]{1,0:T(8,128)(2,1)S(1)}, bf16[128,768]{1,0:T(8,128)(2,1)S(1)}, u32[]{:S(2)}, u32[]{:S(2)}) collective-permute-start(bf16[128,768]{1,0:T(8,128)(2,1)S(1)} %get-tuple-element.79), channel_id=1, source_target_pairs={{24,0},{28,4},{0,8},{4,12},{8,16},{12,20},{16,24},{20,28},{25,1},{... | collective-permute-start | bytes 589832 | tf_op jit(solution)/shard_map/ppermute | solution.py:179
  118.8 18.1 %collective-permute-start.34 = (bf16[128,768]{1,0:T(8,128)(2,1)S(1)}, bf16[128,768]{1,0:T(8,128)(2,1)S(1)}, u32[]{:S(2)}, u32[]{:S(2)}) collective-permute-start(bf16[128,768]{1,0:T(8,128)(2,1)S(1)} %get-tuple-element.80), channel_id=1, source_target_pairs={{28,0},{24,4},{4,8},{0,12},{12,16},{8,20},{20,24},{16,28},{29,1},{... | collective-permute-start | bytes 589832 | tf_op jit(solution)/shard_map/ppermute | solution.py:179

commit v3 on v2

--- a/solution.py
+++ b/solution.py
@@ -10,6 +10,20 @@
 BF16 = jnp.bfloat16
 F32 = jnp.float32
 FREE = pl.CostEstimate(flops=0, bytes_accessed=0, transcendentals=0)
+
+TIES = {
+    "k3": ("k2", "y1"),
+    "y1": ("own", "p0"),
+    "Y0": ("p0",),
+    "y2": ("y1",),
+    "Y1": ("Y0",),
+    "y3": ("y2",),
+    "Y2": ("Y1",),
+    "Y3": ("y3",),
+    "Z2": ("Z0",),
+    "Z3": ("Z1",),
+    "k2": ("k0",),
+}
 
 
 def pick_kernel(places, me, slot, routes_ref, tokens_ref, target_ref, *row_refs):
@@ -109,58 +123,54 @@
     )(*[pltpu.with_memory_space_constraint(one, pltpu.HBM) for one in weights], after)
 
 
-def feed_forward(order, pieces, up, down, after):
-    n, waits = len(pieces), len(after)
-    blocks = [len(piece) for piece in pieces]
-    flat = [block for piece in pieces for block in piece]
-    rows, width = sum(block.shape[0] for block in pieces[0]), flat[0].shape[1]
+def feed_forward(order, near, far, up, down):
+    planes = len(near)
+    rows, width = near[0].shape
     hidden, features = down.shape
-    half = n // 2
 
     def body(order_ref, *refs):
-        piece_refs, up_ref, down_ref = list(refs[: len(flat)]), refs[len(flat)], refs[len(flat) + 1]
-        near_refs, (far_ref, arrived, active) = refs[len(flat) + 2 + waits : -3], refs[-3:]
-        starts = [pl.multiple_of(order_ref[i] * width, 128) for i in range(n)]
-        for i in range(n):
-            at = 0
-            for _ in range(blocks[i]):
-                block = piece_refs.pop(0)
-                arrived[at : at + block.shape[0], pl.ds(starts[i], width)] = block[...]
-                at += block.shape[0]
+        piece_refs, up_ref, down_ref = refs[: 2 * planes], refs[2 * planes], refs[2 * planes + 1]
+        to_near_refs, (to_far_ref, arrived, active) = refs[2 * planes + 2 : -3], refs[-3:]
+        starts = [pl.multiple_of(order_ref[i] * width, 128) for i in range(2 * planes)]
+        for start, piece_ref in zip(starts, piece_refs):
+            arrived[:, pl.ds(start, width)] = piece_ref[...]
         raised = jnp.dot(arrived[...], up_ref[...], preferred_element_type=F32)
         active[...] = (0.5 * raised * (1.0 + jnp.tanh(0.5 * raised))).astype(BF16)
-        for i in reversed(range(n)):
+        for i in reversed(range(2 * planes)):
             value = jnp.dot(active[...], down_ref[:, pl.ds(starts[i], width)], preferred_element_type=F32)
-            if i < half:
-                near_refs[i][...] = value.astype(BF16)
+            if i < planes:
+                to_near_refs[i][...] = value.astype(BF16)
             else:
-                far_ref[i - half] = value.astype(BF16)
+                to_far_ref[i - planes] = value.astype(BF16)
 
     vmem = pl.BlockSpec(memory_space=pltpu.VMEM)
+    out_shape = [jax.ShapeDtypeStruct((rows, width), BF16)] * planes
+    out_shape.append(jax.ShapeDtypeStruct((planes, rows, width), BF16))
     return pl.pallas_call(
         body,
         in_specs=[pl.BlockSpec(memory_space=pltpu.SMEM)]
-        + [vmem] * (len(flat) + 2)
-        + [pl.BlockSpec(memory_space=pl.ANY)] * waits,
-        out_specs=[vmem] * (half + 1),
+        + [vmem] * (2 * planes + 2),
+        out_specs=[vmem] * len(out_shape),
         scratch_shapes=[pltpu.VMEM((rows, features), BF16), pltpu.VMEM((rows, hidden), BF16)],
-        out_shape=[jax.ShapeDtypeStruct((rows, width), BF16)] * half
-        + [jax.ShapeDtypeStruct((half, rows, width), BF16)],
+        out_shape=out_shape,
         compiler_params=pltpu.CompilerParams(vmem_limit_bytes=16 << 20),
-        cost_estimate=FREE,
+        cost_estimate=pl.CostEstimate(
+            flops=4 * rows * hidden * features, bytes_accessed=0, transcendentals=0
+        ),
         name="feed_forward",
-    )(order, *flat, *[pltpu.with_memory_space_constraint(one, pltpu.VMEM) for one in (up, down)], *after)
-
-
-class Lane:
-    def __init__(self, depth):
-        self.depth, self.ended = depth, []
-
-    def send(self, hop, *values):
-        if len(self.ended) >= self.depth:
-            values = lax.optimization_barrier((*values, *self.ended[-self.depth]))[: len(values)]
-        self.ended.append([hop(value) if callable(hop) else hop[i](value) for i, value in enumerate(values)])
-        return self.ended[-1]
+    )(order, *near, *far, *[pltpu.with_memory_space_constraint(one, pltpu.VMEM) for one in (up, down)])
+
+
+class Events:
+    def __init__(self):
+        self.values = {}
+
+    def after(self, name):
+        return [one for event in TIES.get(name, ()) for one in self.values.get(event, [])]
+
+    def hold(self, name, values):
+        after = self.after(name)
+        return list(lax.optimization_barrier((*values, *after))[: len(values)]) if after else list(values)
 
 
 def per_device(tokens, routes, route_gates, up_weight, down_weight):
@@ -172,73 +182,83 @@
     chunks = layers // group
     members = [range(chunk * 2 * group, (chunk + 1) * 2 * group) for chunk in range(chunks)]
     me, rank = lax.axis_index("ep"), lax.axis_index("tp")
-
-    def ep_hop(place, back=False):
+    events = Events()
+
+    def ep_hop(value, place, back=False):
         far, flip = place // 2, place % 2
         pairs = [(i, (i // 2 + far) % layers * 2 + (i % 2 ^ flip)) for i in range(places)]
-        return lambda value: lax.ppermute(value, "ep", [(b, a) for a, b in pairs] if back else pairs)
-
-    def plane_hop(far):
-        pairs = [(i, (i // 2 + far) % planes * 2 + i % 2) for i in range(ranks)]
-        return lambda value: lax.ppermute(value, "tp", pairs)
+        return lax.ppermute(value, "ep", [(b, a) for a, b in pairs] if back else pairs)
+
+    def plane_hop(value, far):
+        return lax.ppermute(value, "tp", [(i, (i // 2 + far) % planes * 2 + i % 2) for i in range(ranks)])
 
     def core_hop(value):
         return lax.ppermute(value, "tp", [(i, i ^ 1) for i in range(ranks)])
 
-    def gather(value):
-        return plane_lane.send([plane_hop(far) for far in range(1, planes)], *[value] * (planes - 1))
+    def gather(name, value):
+        held = events.hold(name, [value])[0]
+        events.values[name] = [plane_hop(held, far) for far in range(1, planes)]
+        return events.values[name]
 
     def join(values):
         return values[0] if len(values) == 1 else jnp.concatenate(values, axis=0)
 
-    plane_lane, out_lane, back_lane = Lane(2), Lane(1), Lane(2)
+    def fetch(name, chunk):
+        away = [place for place in members[chunk] if place > 0]
+        held = events.hold(name, [picked[place] for place in away])
+        events.values[name] = [ep_hop(value, place) for value, place in zip(held, away)]
+        return events.values[name]
+
     order = jnp.stack(
         [(rank // 2 - far) % planes * 2 + rank % 2 for far in range(planes)]
         + [(rank // 2 - far) % planes * 2 + (1 - rank % 2) for far in range(planes)]
     ).astype(jnp.int32)
     target, *picked = pick_rows(routes, tokens, me.reshape(1).astype(jnp.int32), slot, places)
-    pieces, returned = [None] * chunks, [None] * places
-
-    def fetch(chunk):
-        places_of = [place for place in members[chunk] if place > 0]
-        rows = [picked[place] for place in places_of]
-        return out_lane.send([ep_hop(place) for place in places_of], *rows)
+    pieces, totals, outs, returned = [None] * chunks, [None] * chunks, [None] * chunks, [None] * places
 
     def spread(chunk, own, across):
         same_core = [own, *across]
-        pieces[chunk] = [[piece] for piece in same_core + [core_hop(piece) for piece in same_core]]
+        pieces[chunk] = (same_core, [core_hop(piece) for piece in same_core])
 
     def work(chunk):
-        *near, stacked = feed_forward(order, pieces[chunk], up, down, [])
+        *near, stacked = feed_forward(order, *pieces[chunk], up, down)
         crossed = core_hop(stacked)
-        outgoing = [(near[far].astype(F32) + crossed[far].astype(F32)).astype(BF16) for far in range(1, planes)]
-        summed = near[0].astype(F32) + crossed[0].astype(F32)
-        for part in plane_lane.send([plane_hop(planes - far) for far in range(1, planes)], *outgoing):
-            summed = summed + part.astype(F32)
-        results = [summed[i * slot : (i + 1) * slot].astype(BF16) for i in range(len(members[chunk]))]
+        outs[chunk] = [(near[far].astype(F32) + crossed[far].astype(F32)).astype(BF16) for far in range(1, planes)]
+        totals[chunk] = near[0].astype(F32) + crossed[0].astype(F32)
+
+    def reduce(chunk):
+        held = events.hold(f"Y{chunk}", outs[chunk])
+        got = [plane_hop(one, planes - far) for far, one in enumerate(held, 1)]
+        events.values[f"Y{chunk}"] = got
+        for part in got:
+            totals[chunk] = totals[chunk] + part.astype(F32)
+
+    def give(chunk):
+        results = [totals[chunk][i * slot : (i + 1) * slot].astype(BF16) for i in range(len(members[chunk]))]
+        away = [place for place in members[chunk] if place > 0]
         if chunk == 0:
             returned[0] = results.pop(0)
-        away = [place for place in members[chunk] if place > 0]
-        for place, result in zip(away, back_lane.send([ep_hop(place, back=True) for place in away], *results)):
-            returned[place] = result
-
-    home = gather(picked[0])
-    first, out_lane = fetch(0), Lane(1)
-    across = gather(join(first))
-    own = jnp.concatenate([picked[0], *first], axis=0)
-    spread(0, own, [jnp.concatenate(pair, axis=0) for pair in zip(home, across)])
+        held = events.hold(f"Z{chunk}", results)
+        events.values[f"Z{chunk}"] = [ep_hop(one, place, back=True) for one, place in zip(held, away)]
+        for place, one in zip(away, events.values[f"Z{chunk}"]):
+            returned[place] = one
+
+    home = gather("own", picked[0])
+    first = fetch("k0", 0)
+    fetched = {1: join(fetch("k1", 1))}
+    across = gather("p0", join(first))
+    up, down = load([up_weight[0], down_weight[0]], events.values["k1"][0])
+    spread(0, join([picked[0], *first]), [join(pair) for pair in zip(home, across)])
     for chunk in range(chunks):
+        if chunk + 2 < chunks:
+            fetched[chunk + 2] = join(fetch(f"k{chunk + 2}", chunk + 2))
         if chunk + 1 < chunks:
-            own = join(fetch(chunk + 1))
-            if chunk == 0:
-                up, down = load([up_weight[0], down_weight[0]], own)
-                spread(1, own, gather(own))
-                work(0)
-            else:
-                spread(chunk + 1, own, gather(own))
-                work(chunk)
-        else:
-            work(chunk)
+            spread(chunk + 1, fetched[chunk + 1], gather(f"y{chunk + 1}", fetched[chunk + 1]))
+        work(chunk)
+        reduce(chunk)
+        if chunk > 0:
+            give(chunk - 1)
+    give(chunks - 1)
     return combine_rows(target, route_gates, returned, slot)
 
 

time: 140 us -> 123 us (0.88)
  waiting for transfers between devices: 61.4 us -> 35.4 us
  starting transfers between devices: 31.2 us -> 40.4 us
    ppermute x14, waiting for transfers between devices: 39.3 us -> 24.3 us  [ep_hop(): lax.ppermute(value, 'ep', [(b, a) for a, b in pairs] if back else pairs)]
    ppermute x9, waiting for transfers between devices: 22.1 us -> 11.1 us  [plane_hop(): lax.ppermute(value, 'tp', [(i, (i // 2 + far) % planes * 2 + i % 2) for i...]
    ppermute x14, starting transfers between devices: 18.5 us -> 25.6 us  [ep_hop(): lax.ppermute(value, 'ep', [(b, a) for a, b in pairs] if back else pairs)]
    ppermute x9, starting transfers between devices: 10.2 us -> 12.1 us  [plane_hop(): lax.ppermute(value, 'tp', [(i, (i // 2 + far) % planes * 2 + i % 2) for i...]
  transfers between devices with their start and end apart: 35 -> 35, of which waited for: 12 -> 11; matrix products, arithmetic and copies ran while one was open for 2% -> 2% of each run, Pallas kernels for 28% -> 31%
where the time goes in v3:
time: 123 us
  Pallas kernels  42.2 us (34%)
  starting transfers between devices  40.4 us (33%)
  waiting for transfers between devices  35.4 us (29%)
  local copies, waits for them, and re-layouts  3.11 us (3%)
    pallas_call x4, Pallas kernels, feed_forward(): pl.pallas_call(body, in_specs=[pl.BlockSpec(memory_space=pltpu.SMEM)] + [...  30.3 us
    ppermute x14, starting transfers between devices, ep_hop(): lax.ppermute(value, 'ep', [(b, a) for a, b in pairs] if back else pairs)  25.6 us
    ppermute x14, waiting for transfers between devices, ep_hop(): lax.ppermute(value, 'ep', [(b, a) for a, b in pairs] if back else pairs)  24.3 us
    ppermute x9, starting transfers between devices, plane_hop(): lax.ppermute(value, 'tp', [(i, (i // 2 + far) % planes * 2 + i % 2) for i...  12.1 us
    ppermute x9, waiting for transfers between devices, plane_hop(): lax.ppermute(value, 'tp', [(i, (i // 2 + far) % planes * 2 + i % 2) for i...  11.1 us
    pallas_call x1, Pallas kernels, load(): pl.pallas_call(body, in_specs=[pl.BlockSpec(memory_space=pltpu.HBM)] * n...  8.17 us
    unnamed x11, local copies, waits for them, and re-layouts  2.93 us
    ppermute x12, starting transfers between devices, core_hop(): return lax.ppermute(value, 'tp', [(i, i ^ 1) for i in range(ranks)])  2.67 us
  transfers between devices with their start and end apart: 35, of which 11 were waited for; matrix products, arithmetic and copies ran while one was open for 2% of the time, Pallas kernels for 31%

profile of v3, /device:TPU:0, one launch (start us, length us, event | category | flops | bytes accessed | tf_op | source)
XLA Modules:
  0.0 122.6 jit_solution(309772579114916628)
XLA Ops:
  0.0 0.8 copy.6.refs_0_
  0.8 1.0 copy-done
  1.8 1.1 pick_rows.1
  3.0 3.0 %collective-permute-start = (bf16[128,768]{1,0:T(8,128)(2,1)S(1)}, bf16[128,768]{1,0:T(8,128)(2,1)S(1)}, u32[]{:S(2)}, u32[]{:S(2)}) collective-permute-start(bf16[128,768]{1,0:T(8,128)(2,1)S(1)} %get-tuple-element.45), channel_id=1, source_target_pairs={{0,4},{4,0},{8,12},{12,8},{16,20},{20,16},{24,28},{28,24},{1,5},{5... | collective-permute-start | bytes 589832 | tf_op jit(solution)/shard_map/ppermute | solution.py:190
  6.0 1.5 %collective-permute-start.1 = (bf16[128,768]{1,0:T(8,128)(2,1)S(1)}, bf16[128,768]{1,0:T(8,128)(2,1)S(1)}, u32[]{:S(2)}, u32[]{:S(2)}) collective-permute-start(bf16[128,768]{1,0:T(8,128)(2,1)S(1)} %get-tuple-element.44), channel_id=1, source_target_pairs={{0,2},{1,3},{2,0},{3,1},{4,6},{5,7},{6,4},{7,5},{8,10},{9,11},{10,... | collective-permute-start | bytes 589832 | tf_op jit(solution)/shard_map/ppermute | solution.py:193
  7.5 1.6 %collective-permute-start.5 = (bf16[128,768]{1,0:T(8,128)(2,1)S(1)}, bf16[128,768]{1,0:T(8,128)(2,1)S(1)}, u32[]{:S(2)}, u32[]{:S(2)}) collective-permute-start(bf16[128,768]{1,0:T(8,128)(2,1)S(1)} %get-tuple-element.46), channel_id=1, source_target_pairs={{0,8},{4,12},{8,16},{12,20},{16,24},{20,28},{24,0},{28,4},{1,9},{5... | collective-permute-start | bytes 589832 | tf_op jit(solution)/shard_map/ppermute | solution.py:190
  9.1 1.5 %collective-permute-start.9 = (bf16[128,768]{1,0:T(8,128)(2,1)S(1)}, bf16[128,768]{1,0:T(8,128)(2,1)S(1)}, u32[]{:S(2)}, u32[]{:S(2)}) collective-permute-start(bf16[128,768]{1,0:T(8,128)(2,1)S(1)} %get-tuple-element.53), channel_id=1, source_target_pairs={{0,12},{4,8},{8,20},{12,16},{16,28},{20,24},{24,4},{28,0},{1,13},{... | collective-permute-start | bytes 589832 | tf_op jit(solution)/shard_map/ppermute | solution.py:190
  10.6 0.2 collective-permute-done
  11.0 2.9 %collective-permute-start.17 = (bf16[128,768]{1,0:T(8,128)(2,1)S(1)}, bf16[128,768]{1,0:T(8,128)(2,1)}, u32[]{:S(2)}, u32[]{:S(2)}) collective-permute-start(bf16[128,768]{1,0:T(8,128)(2,1)S(1)} %get-tuple-element.61), channel_id=1, source_target_pairs={{0,16},{4,20},{8,24},{12,28},{16,0},{20,4},{24,8},{28,12},{1,17},{... | collective-permute-start | bytes 589832 | tf_op jit(solution)/shard_map/ppermute | solution.py:190
  13.9 1.9 %collective-permute-start.2 = (bf16[128,768]{1,0:T(8,128)(2,1)S(1)}, bf16[128,768]{1,0:T(8,128)(2,1)S(1)}, u32[]{:S(2)}, u32[]{:S(2)}) collective-permute-start(bf16[128,768]{1,0:T(8,128)(2,1)S(1)} %collective-permute-done), channel_id=1, source_target_pairs={{0,2},{1,3},{2,0},{3,1},{4,6},{5,7},{6,4},{7,5},{8,10},{9,11},{10,... | collective-permute-start | bytes 589832 | tf_op jit(solution)/shard_map/ppermute | solution.py:193
  15.8 1.5 %collective-permute-done.5.refs_2_ = bf16[128,768]{1,0:T(8,128)(2,1)S(1)} collective-permute-done((bf16[128,768]{1,0:T(8,128)(2,1)S(1)}, bf16[128,768]{1,0:T(8,128)(2,1)S(1)}, u32[]{:S(2)}, u32[]{:S(2)}) %collective-permute-start.5) | collective-permute-done | bytes 196640 | tf_op jit(solution)/shard_map/ppermute | solution.py:190
  17.3 4.2 %collective-permute-done.9 = bf16[128,768]{1,0:T(8,128)(2,1)S(1)} collective-permute-done((bf16[128,768]{1,0:T(8,128)(2,1)S(1)}, bf16[128,768]{1,0:T(8,128)(2,1)S(1)}, u32[]{:S(2)}, u32[]{:S(2)}) %collective-permute-start.9) | collective-permute-done | bytes 196640 | tf_op jit(solution)/shard_map/ppermute | solution.py:190
  21.4 1.3 %collective-permute-start.10 = (bf16[256,768]{1,0:T(8,128)(2,1)S(1)}, bf16[256,768]{1,0:T(8,128)(2,1)S(1)}, u32[]{:S(2)}, u32[]{:S(2)}) collective-permute-start(bf16[256,768]{1,0:T(8,128)(2,1)S(1)} %constant_dynamic-update-slice_fusion.4.refs_0_), channel_id=1, source_target_pairs={{0,2},{1,3},{2,0},{3,1},{4,6},{5,7},{6,4},{7,5},{8,10},{9,11},{10,... | collective-permute-start | bytes 1179656 | tf_op jit(solution)/shard_map/ppermute | solution.py:193
  22.9 4.7 %collective-permute-start.18 = (bf16[128,768]{1,0:T(8,128)(2,1)S(1)}, bf16[128,768]{1,0:T(8,128)(2,1)S(1)}, u32[]{:S(2)}, u32[]{:S(2)}) collective-permute-start(bf16[128,768]{1,0:T(8,128)(2,1)S(1)} %get-tuple-element.62), channel_id=1, source_target_pairs={{0,20},{4,16},{8,28},{12,24},{16,4},{20,0},{24,12},{28,8},{1,21},{... | collective-permute-start | bytes 589832 | tf_op jit(solution)/shard_map/ppermute | solution.py:190
  27.7 8.2 %load_weights.1 = (bf16[3072,2048]{1,0:T(8,128)(2,1)S(1)}, bf16[2048,3072]{1,0:T(8,128)(2,1)S(1)}) custom-call(bf16[3072,2048]{1,0:T(8,128)(2,1)} %bitcast.47, bf16[2048,3072]{1,0:T(8,128)(2,1)} %bitcast.48, bf16[128,768]{1,0:T(8,128)(2,1)S(1)} %collective-permute-done.5.refs_2_), custom_call_target="tpu_custom_call" | custom-call | tf_op jit(solution)/shard_map/load_weights/pallas_call | solution.py:114
  35.9 0.1 collective-permute-start.11
  36.0 0.9 constant_dynamic-update-slice_fusion.7
  37.0 0.3 collective-permute-done.18
  37.3 2.1 %collective-permute-start.19 = (bf16[256,768]{1,0:T(8,128)(2,1)S(1)}, bf16[256,768]{1,0:T(8,128)(2,1)S(1)}, u32[]{:S(2)}, u32[]{:S(2)}) collective-permute-start(bf16[256,768]{1,0:T(8,128)(2,1)S(1)} %constant_dynamic-update-slice_fusion.6.refs_0_), channel_id=1, source_target_pairs={{0,2},{1,3},{2,0},{3,1},{4,6},{5,7},{6,4},{7,5},{8,10},{9,11},{10,... | collective-permute-start | bytes 1179656 | tf_op jit(solution)/shard_map/ppermute | solution.py:193
  39.3 1.5 %collective-permute-start.27 = (bf16[128,768]{1,0:T(8,128)(2,1)S(1)}, bf16[128,768]{1,0:T(8,128)(2,1)S(1)}, u32[]{:S(2)}, u32[]{:S(2)}) collective-permute-start(bf16[128,768]{1,0:T(8,128)(2,1)S(1)} %get-tuple-element.73), channel_id=1, source_target_pairs={{0,28},{4,24},{8,4},{12,0},{16,12},{20,8},{24,20},{28,16},{1,29},{... | collective-permute-start | bytes 589832 | tf_op jit(solution)/shard_map/ppermute | solution.py:190
  40.8 7.5 %feed_forward.4 = (bf16[256,768]{1,0:T(8,128)(2,1)S(1)}, bf16[256,768]{1,0:T(8,128)(2,1)S(1)}, bf16[2,256,768]{2,1,0:T(8,128)(2,1)S(1)}) custom-call(s32[4]{0:T(128)S(1)} %pad_add_fusion.order_ref, bf16[256,768]{1,0:T(8,128)(2,1)S(1)} %constant_dynamic-update-slice_fusion.refs_0_, bf16[256,768]{1,0:T(8,128)(2,1)S(1)} %constant_dynamic-update-slice_fusion.2.refs_1_, ...), custom_call_target="tpu_custom_call" | custom-call | flops 6442450944 | tf_op jit(solution)/shard_map/feed_forward/pallas_call | solution.py:149
  48.4 0.6 collective-permute-start.6
  48.9 1.0 collective-permute-done.27
  49.9 0.6 collective-permute-start.29
  50.5 0.3 collective-permute-start.28
  50.9 7.5 %feed_forward.5 = (bf16[256,768]{1,0:T(8,128)(2,1)S(1)}, bf16[256,768]{1,0:T(8,128)(2,1)S(1)}, bf16[2,256,768]{2,1,0:T(8,128)(2,1)S(1)}) custom-call(s32[4]{0:T(128)S(1)} %pad_add_fusion.order_ref, bf16[256,768]{1,0:T(8,128)(2,1)S(1)} %constant_dynamic-update-slice_fusion.4.refs_0_, bf16[256,768]{1,0:T(8,128)(2,1)S(1)} %collective-permute-done.10.refs_1_, ...), custom_call_target="tpu_custom_call" | custom-call | flops 6442450944 | tf_op jit(solution)/shard_map/feed_forward/pallas_call | solution.py:149
  58.4 0.6 collective-permute-start.13
  59.1 1.7 %collective-permute-start.7 = (bf16[256,768]{1,0:T(8,128)(2,1)S(1)}, bf16[256,768]{1,0:T(8,128)(2,1)S(1)}, u32[]{:S(2)}, u32[]{:S(2)}) collective-permute-start(bf16[256,768]{1,0:T(8,128)(2,1)S(1)} %fusion.9), channel_id=1, source_target_pairs={{0,2},{1,3},{2,0},{3,1},{4,6},{5,7},{6,4},{7,5},{8,10},{9,11},{10,... | collective-permute-start | bytes 1179656 | tf_op jit(solution)/shard_map/ppermute | solution.py:193
  60.8 0.8 collective-permute-done.28.refs_1_
  61.6 7.7 %feed_forward.6 = (bf16[256,768]{1,0:T(8,128)(2,1)S(1)}, bf16[256,768]{1,0:T(8,128)(2,1)S(1)}, bf16[2,256,768]{2,1,0:T(8,128)(2,1)S(1)}) custom-call(s32[4]{0:T(128)S(1)} %pad_add_fusion.order_ref, bf16[256,768]{1,0:T(8,128)(2,1)S(1)} %constant_dynamic-update-slice_fusion.6.refs_0_, bf16[256,768]{1,0:T(8,128)(2,1)S(1)} %collective-permute-done.19.refs_1_, ...), custom_call_target="tpu_custom_call" | custom-call | flops 6442450944 | tf_op jit(solution)/shard_map/feed_forward/pallas_call | solution.py:149
  69.4 0.6 collective-permute-start.22
  70.2 1.7 %collective-permute-start.14 = (bf16[256,768]{1,0:T(8,128)(2,1)S(1)}, bf16[256,768]{1,0:T(8,128)(2,1)S(1)}, u32[]{:S(2)}, u32[]{:S(2)}) collective-permute-start(bf16[256,768]{1,0:T(8,128)(2,1)S(1)} %fusion.6), channel_id=1, source_target_pairs={{0,2},{1,3},{2,0},{3,1},{4,6},{5,7},{6,4},{7,5},{8,10},{9,11},{10,... | collective-permute-start | bytes 1179656 | tf_op jit(solution)/shard_map/ppermute | solution.py:193
  71.9 7.5 %feed_forward.7 = (bf16[256,768]{1,0:T(8,128)(2,1)S(1)}, bf16[256,768]{1,0:T(8,128)(2,1)S(1)}, bf16[2,256,768]{2,1,0:T(8,128)(2,1)S(1)}) custom-call(s32[4]{0:T(128)S(1)} %pad_add_fusion.order_ref, bf16[256,768]{1,0:T(8,128)(2,1)S(1)} %constant_dynamic-update-slice_fusion.8.refs_0_, bf16[256,768]{1,0:T(8,128)(2,1)S(1)} %collective-permute-done.28.refs_1_, ...), custom_call_target="tpu_custom_call" | custom-call | flops 6442450944 | tf_op jit(solution)/shard_map/feed_forward/pallas_call | solution.py:149
  79.6 1.9 %collective-permute-start.8 = (bf16[128,768]{1,0:T(8,128)(2,1)S(1)}, bf16[128,768]{1,0:T(8,128)(2,1)S(1)}, u32[]{:S(2)}, u32[]{:S(2)}) collective-permute-start(bf16[128,768]{1,0:T(8,128)(2,1)S(1)} %get-tuple-element.87), channel_id=1, source_target_pairs={{4,0},{0,4},{12,8},{8,12},{20,16},{16,20},{28,24},{24,28},{5,1},{1... | collective-permute-start | bytes 589832 | tf_op jit(solution)/shard_map/ppermute | solution.py:190
  81.6 0.4 collective-permute-start.23
  82.0 0.2 fusion.8
  82.2 2.6 %collective-permute-start.15 = (bf16[128,768]{1,0:T(8,128)(2,1)S(1)}, bf16[128,768]{1,0:T(8,128)(2,1)S(1)}, u32[]{:S(2)}, u32[]{:S(2)}) collective-permute-start(bf16[128,768]{1,0:T(8,128)(2,1)S(1)} %get-tuple-element.86), channel_id=1, source_target_pairs={{8,0},{12,4},{16,8},{20,12},{24,16},{28,20},{0,24},{4,28},{9,1},{1... | collective-permute-start | bytes 589832 | tf_op jit(solution)/shard_map/ppermute | solution.py:190
  84.9 0.9 collective-permute-start.16
  85.9 1.2 %collective-permute-start.32 = (bf16[256,768]{1,0:T(8,128)(2,1)S(1)}, bf16[256,768]{1,0:T(8,128)(2,1)S(1)}, u32[]{:S(2)}, u32[]{:S(2)}) collective-permute-start(bf16[256,768]{1,0:T(8,128)(2,1)S(1)} %fusion), channel_id=1, source_target_pairs={{0,2},{1,3},{2,0},{3,1},{4,6},{5,7},{6,4},{7,5},{8,10},{9,11},{10,... | collective-permute-start | bytes 1179656 | tf_op jit(solution)/shard_map/ppermute | solution.py:193
  87.1 6.5 %collective-permute-done.23 = bf16[256,768]{1,0:T(8,128)(2,1)S(1)} collective-permute-done((bf16[256,768]{1,0:T(8,128)(2,1)S(1)}, bf16[256,768]{1,0:T(8,128)(2,1)S(1)}, u32[]{:S(2)}, u32[]{:S(2)}) %collective-permute-start.23) | collective-permute-done | bytes 393248 | tf_op jit(solution)/shard_map/ppermute | solution.py:193
  93.6 0.2 fusion.5
  93.9 0.9 collective-permute-start.24
  94.7 3.0 %collective-permute-start.25 = (bf16[128,768]{1,0:T(8,128)(2,1)S(1)}, bf16[128,768]{1,0:T(8,128)(2,1)S(1)}, u32[]{:S(2)}, u32[]{:S(2)}) collective-permute-start(bf16[128,768]{1,0:T(8,128)(2,1)S(1)} %get-tuple-element.69), channel_id=1, source_target_pairs={{20,0},{16,4},{28,8},{24,12},{4,16},{0,20},{12,24},{8,28},{21,1},{... | collective-permute-start | bytes 589832 | tf_op jit(solution)/shard_map/ppermute | solution.py:190
  97.7 3.7 %collective-permute-done.32 = bf16[256,768]{1,0:T(8,128)(2,1)S(1)} collective-permute-done((bf16[256,768]{1,0:T(8,128)(2,1)S(1)}, bf16[256,768]{1,0:T(8,128)(2,1)S(1)}, u32[]{:S(2)}, u32[]{:S(2)}) %collective-permute-start.32) | collective-permute-done | bytes 393248 | tf_op jit(solution)/shard_map/ppermute | solution.py:193
  101.6 1.1 collective-permute-start.34
  102.8 13.8 %collective-permute-done.24.refs_4_ = bf16[128,768]{1,0:T(8,128)(2,1)S(1)} collective-permute-done((bf16[128,768]{1,0:T(8,128)(2,1)S(1)}, bf16[128,768]{1,0:T(8,128)(2,1)S(1)}, u32[]{:S(2)}, u32[]{:S(2)}) %collective-permute-start.24) | collective-permute-done | bytes 196640 | tf_op jit(solution)/shard_map/ppermute | solution.py:190
  116.7 3.3 %collective-permute-done.25.refs_5_ = bf16[128,768]{1,0:T(8,128)(2,1)S(1)} collective-permute-done((bf16[128,768]{1,0:T(8,128)(2,1)S(1)}, bf16[128,768]{1,0:T(8,128)(2,1)S(1)}, u32[]{:S(2)}, u32[]{:S(2)}) %collective-permute-start.25) | collective-permute-done | bytes 196640 | tf_op jit(solution)/shard_map/ppermute | solution.py:190
  120.0 2.6 %combine_rows.1 = bf16[256,768]{1,0:T(8,128)(2,1)} custom-call(s32[256,2]{1,0:T(8,128)S(1)} %get-tuple-element.43.target_ref, f32[256,2]{1,0:T(8,128)S(1)} %copy.7.gates_ref, bf16[128,768]{1,0:T(8,128)(2,1)S(1)} %get-tuple-element.88.refs_0_, bf16[128,768]{1,0:T(8,128)(2,1)S(1)} %collective-permute-done.8.refs_1_, ...), custom_call_target="tpu_custom_call" | custom-call | tf_op jit(solution)/shard_map/combine_rows/pallas_call | solution.py:93
  (58 shorter events, 1.6 us)
Async XLA Ops:
  0.8 1.0 copy-start
  3.0 7.9 %collective-permute-start = (bf16[128,768]{1,0:T(8,128)(2,1)S(1)}, bf16[128,768]{1,0:T(8,128)(2,1)S(1)}, u32[]{:S(2)}, u32[]{:S(2)}) collective-permute-start(bf16[128,768]{1,0:T(8,128)(2,1)S(1)} %get-tuple-element.45), channel_id=1, source_target_pairs={{0,4},{4,0},{8,12},{12,8},{16,20},{20,16},{24,28},{28,24},{1,5},{5... | collective-permute-start | bytes 589832 | tf_op jit(solution)/shard_map/ppermute | solution.py:190
  6.0 7.9 %collective-permute-start.1 = (bf16[128,768]{1,0:T(8,128)(2,1)S(1)}, bf16[128,768]{1,0:T(8,128)(2,1)S(1)}, u32[]{:S(2)}, u32[]{:S(2)}) collective-permute-start(bf16[128,768]{1,0:T(8,128)(2,1)S(1)} %get-tuple-element.44), channel_id=1, source_target_pairs={{0,2},{1,3},{2,0},{3,1},{4,6},{5,7},{6,4},{7,5},{8,10},{9,11},{10,... | collective-permute-start | bytes 589832 | tf_op jit(solution)/shard_map/ppermute | solution.py:193
  7.5 9.7 %collective-permute-start.5 = (bf16[128,768]{1,0:T(8,128)(2,1)S(1)}, bf16[128,768]{1,0:T(8,128)(2,1)S(1)}, u32[]{:S(2)}, u32[]{:S(2)}) collective-permute-start(bf16[128,768]{1,0:T(8,128)(2,1)S(1)} %get-tuple-element.46), channel_id=1, source_target_pairs={{0,8},{4,12},{8,16},{12,20},{16,24},{20,28},{24,0},{28,4},{1,9},{5... | collective-permute-start | bytes 589832 | tf_op jit(solution)/shard_map/ppermute | solution.py:190
  9.1 12.3 %collective-permute-start.9 = (bf16[128,768]{1,0:T(8,128)(2,1)S(1)}, bf16[128,768]{1,0:T(8,128)(2,1)S(1)}, u32[]{:S(2)}, u32[]{:S(2)}) collective-permute-start(bf16[128,768]{1,0:T(8,128)(2,1)S(1)} %get-tuple-element.53), channel_id=1, source_target_pairs={{0,12},{4,8},{8,20},{12,16},{16,28},{20,24},{24,4},{28,0},{1,13},{... | collective-permute-start | bytes 589832 | tf_op jit(solution)/shard_map/ppermute | solution.py:190
  10.9 28.4 %collective-permute-start.3 = (bf16[256,768]{1,0:T(8,128)(2,1)S(1)}, bf16[256,768]{1,0:T(8,128)(2,1)S(1)}, u32[]{:S(2)}, u32[]{:S(2)}) collective-permute-start(bf16[256,768]{1,0:T(8,128)(2,1)S(1)} %constant_dynamic-update-slice_fusion.refs_0_), channel_id=1, source_target_pairs={{0,1},{1,0},{2,3},{3,2},{4,5},{5,4},{6,7},{7,6},{8,9},{9,8},{10,11... | collective-permute-start | bytes 1179656 | tf_op jit(solution)/shard_map/ppermute | solution.py:196
  11.0 24.9 %collective-permute-start.17 = (bf16[128,768]{1,0:T(8,128)(2,1)S(1)}, bf16[128,768]{1,0:T(8,128)(2,1)}, u32[]{:S(2)}, u32[]{:S(2)}) collective-permute-start(bf16[128,768]{1,0:T(8,128)(2,1)S(1)} %get-tuple-element.61), channel_id=1, source_target_pairs={{0,16},{4,20},{8,24},{12,28},{16,0},{20,4},{24,8},{28,12},{1,17},{... | collective-permute-start | bytes 589832 | tf_op jit(solution)/shard_map/ppermute | solution.py:190
  13.9 7.6 %collective-permute-start.2 = (bf16[128,768]{1,0:T(8,128)(2,1)S(1)}, bf16[128,768]{1,0:T(8,128)(2,1)S(1)}, u32[]{:S(2)}, u32[]{:S(2)}) collective-permute-start(bf16[128,768]{1,0:T(8,128)(2,1)S(1)} %collective-permute-done), channel_id=1, source_target_pairs={{0,2},{1,3},{2,0},{3,1},{4,6},{5,7},{6,4},{7,5},{8,10},{9,11},{10,... | collective-permute-start | bytes 589832 | tf_op jit(solution)/shard_map/ppermute | solution.py:193
  21.4 15.8 %collective-permute-start.10 = (bf16[256,768]{1,0:T(8,128)(2,1)S(1)}, bf16[256,768]{1,0:T(8,128)(2,1)S(1)}, u32[]{:S(2)}, u32[]{:S(2)}) collective-permute-start(bf16[256,768]{1,0:T(8,128)(2,1)S(1)} %constant_dynamic-update-slice_fusion.4.refs_0_), channel_id=1, source_target_pairs={{0,2},{1,3},{2,0},{3,1},{4,6},{5,7},{6,4},{7,5},{8,10},{9,11},{10,... | collective-permute-start | bytes 1179656 | tf_op jit(solution)/shard_map/ppermute | solution.py:193
  22.7 18.1 %collective-permute-start.4 = (bf16[256,768]{1,0:T(8,128)(2,1)S(1)}, bf16[256,768]{1,0:T(8,128)(2,1)S(1)}, u32[]{:S(2)}, u32[]{:S(2)}) collective-permute-start(bf16[256,768]{1,0:T(8,128)(2,1)S(1)} %constant_dynamic-update-slice_fusion.2.refs_1_), channel_id=1, source_target_pairs={{0,1},{1,0},{2,3},{3,2},{4,5},{5,4},{6,7},{7,6},{8,9},{9,8},{10,11... | collective-permute-start | bytes 1179656 | tf_op jit(solution)/shard_map/ppermute | solution.py:196
  22.9 14.4 %collective-permute-start.18 = (bf16[128,768]{1,0:T(8,128)(2,1)S(1)}, bf16[128,768]{1,0:T(8,128)(2,1)S(1)}, u32[]{:S(2)}, u32[]{:S(2)}) collective-permute-start(bf16[128,768]{1,0:T(8,128)(2,1)S(1)} %get-tuple-element.62), channel_id=1, source_target_pairs={{0,20},{4,16},{8,28},{12,24},{16,4},{20,0},{24,12},{28,8},{1,21},{... | collective-permute-start | bytes 589832 | tf_op jit(solution)/shard_map/ppermute | solution.py:190
  35.9 14.6 %collective-permute-start.11 = (bf16[256,768]{1,0:T(8,128)(2,1)S(1)}, bf16[256,768]{1,0:T(8,128)(2,1)S(1)}, u32[]{:S(2)}, u32[]{:S(2)}) collective-permute-start(bf16[256,768]{1,0:T(8,128)(2,1)S(1)} %constant_dynamic-update-slice_fusion.4.refs_0_), channel_id=1, source_target_pairs={{0,1},{1,0},{2,3},{3,2},{4,5},{5,4},{6,7},{7,6},{8,9},{9,8},{10,11... | collective-permute-start | bytes 1179656 | tf_op jit(solution)/shard_map/ppermute | solution.py:196
  37.3 12.7 %collective-permute-start.19 = (bf16[256,768]{1,0:T(8,128)(2,1)S(1)}, bf16[256,768]{1,0:T(8,128)(2,1)S(1)}, u32[]{:S(2)}, u32[]{:S(2)}) collective-permute-start(bf16[256,768]{1,0:T(8,128)(2,1)S(1)} %constant_dynamic-update-slice_fusion.6.refs_0_), channel_id=1, source_target_pairs={{0,2},{1,3},{2,0},{3,1},{4,6},{5,7},{6,4},{7,5},{8,10},{9,11},{10,... | collective-permute-start | bytes 1179656 | tf_op jit(solution)/shard_map/ppermute | solution.py:193
  39.3 9.0 %collective-permute-start.26 = (bf16[128,768]{1,0:T(8,128)(2,1)S(1)}, bf16[128,768]{1,0:T(8,128)(2,1)S(1)}, u32[]{:S(2)}, u32[]{:S(2)}) collective-permute-start(bf16[128,768]{1,0:T(8,128)(2,1)S(1)} %get-tuple-element.72), channel_id=1, source_target_pairs={{0,24},{4,28},{8,0},{12,4},{16,8},{20,12},{24,16},{28,20},{1,25},{... | collective-permute-start | bytes 589832 | tf_op jit(solution)/shard_map/ppermute | solution.py:190
  39.3 10.6 %collective-permute-start.27 = (bf16[128,768]{1,0:T(8,128)(2,1)S(1)}, bf16[128,768]{1,0:T(8,128)(2,1)S(1)}, u32[]{:S(2)}, u32[]{:S(2)}) collective-permute-start(bf16[128,768]{1,0:T(8,128)(2,1)S(1)} %get-tuple-element.73), channel_id=1, source_target_pairs={{0,28},{4,24},{8,4},{12,0},{16,12},{20,8},{24,20},{28,16},{1,29},{... | collective-permute-start | bytes 589832 | tf_op jit(solution)/shard_map/ppermute | solution.py:190
  40.8 10.0 %collective-permute-start.12 = (bf16[256,768]{1,0:T(8,128)(2,1)S(1)}, bf16[256,768]{1,0:T(8,128)(2,1)S(1)}, u32[]{:S(2)}, u32[]{:S(2)}) collective-permute-start(bf16[256,768]{1,0:T(8,128)(2,1)S(1)} %collective-permute-done.10.refs_1_), channel_id=1, source_target_pairs={{0,1},{1,0},{2,3},{3,2},{4,5},{5,4},{6,7},{7,6},{8,9},{9,8},{10,11... | collective-permute-start | bytes 1179656 | tf_op jit(solution)/shard_map/ppermute | solution.py:196
  48.4 10.0 %collective-permute-start.6 = (bf16[2,256,768]{2,1,0:T(8,128)(2,1)S(1)}, bf16[2,256,768]{2,1,0:T(8,128)(2,1)S(1)}, u32[]{:S(2)}, u32[]{:S(2)}) collective-permute-start(bf16[2,256,768]{2,1,0:T(8,128)(2,1)S(1)} %get-tuple-element.50), channel_id=1, source_target_pairs={{0,1},{1,0},{2,3},{3,2},{4,5},{5,4},{6,7},{7,6},{8,9},{9,8},{10,11... | collective-permute-start | bytes 2359304 | tf_op jit(solution)/shard_map/ppermute | solution.py:196
  49.9 9.2 %collective-permute-start.20 = (bf16[256,768]{1,0:T(8,128)(2,1)S(1)}, bf16[256,768]{1,0:T(8,128)(2,1)S(1)}, u32[]{:S(2)}, u32[]{:S(2)}) collective-permute-start(bf16[256,768]{1,0:T(8,128)(2,1)S(1)} %constant_dynamic-update-slice_fusion.6.refs_0_), channel_id=1, source_target_pairs={{0,1},{1,0},{2,3},{3,2},{4,5},{5,4},{6,7},{7,6},{8,9},{9,8},{10,11... | collective-permute-start | bytes 1179656 | tf_op jit(solution)/shard_map/ppermute | solution.py:196
  49.9 21.9 %collective-permute-start.29 = (bf16[256,768]{1,0:T(8,128)(2,1)S(1)}, bf16[256,768]{1,0:T(8,128)(2,1)S(1)}, u32[]{:S(2)}, u32[]{:S(2)}) collective-permute-start(bf16[256,768]{1,0:T(8,128)(2,1)S(1)} %constant_dynamic-update-slice_fusion.8.refs_0_), channel_id=1, source_target_pairs={{0,1},{1,0},{2,3},{3,2},{4,5},{5,4},{6,7},{7,6},{8,9},{9,8},{10,11... | collective-permute-start | bytes 1179656 | tf_op jit(solution)/shard_map/ppermute | solution.py:196
  50.5 11.1 %collective-permute-start.28 = (bf16[256,768]{1,0:T(8,128)(2,1)S(1)}, bf16[256,768]{1,0:T(8,128)(2,1)S(1)}, u32[]{:S(2)}, u32[]{:S(2)}) collective-permute-start(bf16[256,768]{1,0:T(8,128)(2,1)S(1)} %constant_dynamic-update-slice_fusion.8.refs_0_), channel_id=1, source_target_pairs={{0,2},{1,3},{2,0},{3,1},{4,6},{5,7},{6,4},{7,5},{8,10},{9,11},{10,... | collective-permute-start | bytes 1179656 | tf_op jit(solution)/shard_map/ppermute | solution.py:193
  50.9 10.8 %collective-permute-start.21 = (bf16[256,768]{1,0:T(8,128)(2,1)S(1)}, bf16[256,768]{1,0:T(8,128)(2,1)S(1)}, u32[]{:S(2)}, u32[]{:S(2)}) collective-permute-start(bf16[256,768]{1,0:T(8,128)(2,1)S(1)} %collective-permute-done.19.refs_1_), channel_id=1, source_target_pairs={{0,1},{1,0},{2,3},{3,2},{4,5},{5,4},{6,7},{7,6},{8,9},{9,8},{10,11... | collective-permute-start | bytes 1179656 | tf_op jit(solution)/shard_map/ppermute | solution.py:196
  58.4 11.6 %collective-permute-start.13 = (bf16[2,256,768]{2,1,0:T(8,128)(2,1)S(1)}, bf16[2,256,768]{2,1,0:T(8,128)(2,1)S(1)}, u32[]{:S(2)}, u32[]{:S(2)}) collective-permute-start(bf16[2,256,768]{2,1,0:T(8,128)(2,1)S(1)} %get-tuple-element.56), channel_id=1, source_target_pairs={{0,1},{1,0},{2,3},{3,2},{4,5},{5,4},{6,7},{7,6},{8,9},{9,8},{10,11... | collective-permute-start | bytes 2359304 | tf_op jit(solution)/shard_map/ppermute | solution.py:196
  59.1 11.1 %collective-permute-start.7 = (bf16[256,768]{1,0:T(8,128)(2,1)S(1)}, bf16[256,768]{1,0:T(8,128)(2,1)S(1)}, u32[]{:S(2)}, u32[]{:S(2)}) collective-permute-start(bf16[256,768]{1,0:T(8,128)(2,1)S(1)} %fusion.9), channel_id=1, source_target_pairs={{0,2},{1,3},{2,0},{3,1},{4,6},{5,7},{6,4},{7,5},{8,10},{9,11},{10,... | collective-permute-start | bytes 1179656 | tf_op jit(solution)/shard_map/ppermute | solution.py:193
  61.6 10.2 %collective-permute-start.30 = (bf16[256,768]{1,0:T(8,128)(2,1)S(1)}, bf16[256,768]{1,0:T(8,128)(2,1)S(1)}, u32[]{:S(2)}, u32[]{:S(2)}) collective-permute-start(bf16[256,768]{1,0:T(8,128)(2,1)S(1)} %collective-permute-done.28.refs_1_), channel_id=1, source_target_pairs={{0,1},{1,0},{2,3},{3,2},{4,5},{5,4},{6,7},{7,6},{8,9},{9,8},{10,11... | collective-permute-start | bytes 1179656 | tf_op jit(solution)/shard_map/ppermute | solution.py:196
  69.4 12.1 %collective-permute-start.22 = (bf16[2,256,768]{2,1,0:T(8,128)(2,1)S(1)}, bf16[2,256,768]{2,1,0:T(8,128)(2,1)S(1)}, u32[]{:S(2)}, u32[]{:S(2)}) collective-permute-start(bf16[2,256,768]{2,1,0:T(8,128)(2,1)S(1)} %get-tuple-element.65), channel_id=1, source_target_pairs={{0,1},{1,0},{2,3},{3,2},{4,5},{5,4},{6,7},{7,6},{8,9},{9,8},{10,11... | collective-permute-start | bytes 2359304 | tf_op jit(solution)/shard_map/ppermute | solution.py:196
  70.0 32.6 %copy-start.1 = (f32[256,2]{0,1:T(2,128)S(1)}, f32[256,2]{0,1:T(2,128)}, u32[]{:S(2)}) copy-start(f32[256,2]{0,1:T(2,128)} %param.7) | copy-start | bytes 6148
  70.2 11.4 %collective-permute-start.14 = (bf16[256,768]{1,0:T(8,128)(2,1)S(1)}, bf16[256,768]{1,0:T(8,128)(2,1)S(1)}, u32[]{:S(2)}, u32[]{:S(2)}) collective-permute-start(bf16[256,768]{1,0:T(8,128)(2,1)S(1)} %fusion.6), channel_id=1, source_target_pairs={{0,2},{1,3},{2,0},{3,1},{4,6},{5,7},{6,4},{7,5},{8,10},{9,11},{10,... | collective-permute-start | bytes 1179656 | tf_op jit(solution)/shard_map/ppermute | solution.py:193
  79.4 6.4 %collective-permute-start.31 = (bf16[2,256,768]{2,1,0:T(8,128)(2,1)S(1)}, bf16[2,256,768]{2,1,0:T(8,128)(2,1)S(1)}, u32[]{:S(2)}, u32[]{:S(2)}) collective-permute-start(bf16[2,256,768]{2,1,0:T(8,128)(2,1)S(1)} %get-tuple-element.76), channel_id=1, source_target_pairs={{0,1},{1,0},{2,3},{3,2},{4,5},{5,4},{6,7},{7,6},{8,9},{9,8},{10,11... | collective-permute-start | bytes 2359304 | tf_op jit(solution)/shard_map/ppermute | solution.py:196
  79.6 14.2 %collective-permute-start.8 = (bf16[128,768]{1,0:T(8,128)(2,1)S(1)}, bf16[128,768]{1,0:T(8,128)(2,1)S(1)}, u32[]{:S(2)}, u32[]{:S(2)}) collective-permute-start(bf16[128,768]{1,0:T(8,128)(2,1)S(1)} %get-tuple-element.87), channel_id=1, source_target_pairs={{4,0},{0,4},{12,8},{8,12},{20,16},{16,20},{28,24},{24,28},{5,1},{1... | collective-permute-start | bytes 589832 | tf_op jit(solution)/shard_map/ppermute | solution.py:190
  81.6 12.0 %collective-permute-start.23 = (bf16[256,768]{1,0:T(8,128)(2,1)S(1)}, bf16[256,768]{1,0:T(8,128)(2,1)S(1)}, u32[]{:S(2)}, u32[]{:S(2)}) collective-permute-start(bf16[256,768]{1,0:T(8,128)(2,1)S(1)} %fusion.3), channel_id=1, source_target_pairs={{0,2},{1,3},{2,0},{3,1},{4,6},{5,7},{6,4},{7,5},{8,10},{9,11},{10,... | collective-permute-start | bytes 1179656 | tf_op jit(solution)/shard_map/ppermute | solution.py:193
  82.2 19.3 %collective-permute-start.15 = (bf16[128,768]{1,0:T(8,128)(2,1)S(1)}, bf16[128,768]{1,0:T(8,128)(2,1)S(1)}, u32[]{:S(2)}, u32[]{:S(2)}) collective-permute-start(bf16[128,768]{1,0:T(8,128)(2,1)S(1)} %get-tuple-element.86), channel_id=1, source_target_pairs={{8,0},{12,4},{16,8},{20,12},{24,16},{28,20},{0,24},{4,28},{9,1},{1... | collective-permute-start | bytes 589832 | tf_op jit(solution)/shard_map/ppermute | solution.py:190
  84.9 16.7 %collective-permute-start.16 = (bf16[128,768]{1,0:T(8,128)(2,1)S(1)}, bf16[128,768]{1,0:T(8,128)(2,1)S(1)}, u32[]{:S(2)}, u32[]{:S(2)}) collective-permute-start(bf16[128,768]{1,0:T(8,128)(2,1)S(1)} %get-tuple-element.85), channel_id=1, source_target_pairs={{12,0},{8,4},{20,8},{16,12},{28,16},{24,20},{4,24},{0,28},{13,1},{... | collective-permute-start | bytes 589832 | tf_op jit(solution)/shard_map/ppermute | solution.py:190
  85.9 15.4 %collective-permute-start.32 = (bf16[256,768]{1,0:T(8,128)(2,1)S(1)}, bf16[256,768]{1,0:T(8,128)(2,1)S(1)}, u32[]{:S(2)}, u32[]{:S(2)}) collective-permute-start(bf16[256,768]{1,0:T(8,128)(2,1)S(1)} %fusion), channel_id=1, source_target_pairs={{0,2},{1,3},{2,0},{3,1},{4,6},{5,7},{6,4},{7,5},{8,10},{9,11},{10,... | collective-permute-start | bytes 1179656 | tf_op jit(solution)/shard_map/ppermute | solution.py:193
  93.9 22.8 %collective-permute-start.24 = (bf16[128,768]{1,0:T(8,128)(2,1)S(1)}, bf16[128,768]{1,0:T(8,128)(2,1)S(1)}, u32[]{:S(2)}, u32[]{:S(2)}) collective-permute-start(bf16[128,768]{1,0:T(8,128)(2,1)S(1)} %get-tuple-element.68), channel_id=1, source_target_pairs={{16,0},{20,4},{24,8},{28,12},{0,16},{4,20},{8,24},{12,28},{17,1},{... | collective-permute-start | bytes 589832 | tf_op jit(solution)/shard_map/ppermute | solution.py:190
  94.7 25.3 %collective-permute-start.25 = (bf16[128,768]{1,0:T(8,128)(2,1)S(1)}, bf16[128,768]{1,0:T(8,128)(2,1)S(1)}, u32[]{:S(2)}, u32[]{:S(2)}) collective-permute-start(bf16[128,768]{1,0:T(8,128)(2,1)S(1)} %get-tuple-element.69), channel_id=1, source_target_pairs={{20,0},{16,4},{28,8},{24,12},{4,16},{0,20},{12,24},{8,28},{21,1},{... | collective-permute-start | bytes 589832 | tf_op jit(solution)/shard_map/ppermute | solution.py:190
  101.5 18.5 %collective-permute-start.33 = (bf16[128,768]{1,0:T(8,128)(2,1)S(1)}, bf16[128,768]{1,0:T(8,128)(2,1)S(1)}, u32[]{:S(2)}, u32[]{:S(2)}) collective-permute-start(bf16[128,768]{1,0:T(8,128)(2,1)S(1)} %get-tuple-element.79), channel_id=1, source_target_pairs={{24,0},{28,4},{0,8},{4,12},{8,16},{12,20},{16,24},{20,28},{25,1},{... | collective-permute-start | bytes 589832 | tf_op jit(solution)/shard_map/ppermute | solution.py:190
  101.6 18.4 %collective-permute-start.34 = (bf16[128,768]{1,0:T(8,128)(2,1)S(1)}, bf16[128,768]{1,0:T(8,128)(2,1)S(1)}, u32[]{:S(2)}, u32[]{:S(2)}) collective-permute-start(bf16[128,768]{1,0:T(8,128)(2,1)S(1)} %get-tuple-element.80), channel_id=1, source_target_pairs={{28,0},{24,4},{4,8},{0,12},{12,16},{8,20},{20,24},{16,28},{29,1},{... | collective-permute-start | bytes 589832 | tf_op jit(solution)/shard_map/ppermute | solution.py:190
